TPU v7x, 512 devices: a whole 4x4x16 slice. The times are simulated.
512 devices in a mesh: band: 4 (over y), gx: 16 (over z), gy: 8 (over x, core).
Axes of the slice: x: 4, y: 4, z: 16, core: 2. Of those that a mesh axis runs over, the one named last changes fastest.
Arguments:
- psi_coeff: float32 [8, 256, 256, 256], P('band', 'gx', 'gy'), parts along dimension 0, may hold values from -6 to 6
- potential: float32 [256, 256, 256], P(('gx', 'gy')), may hold values from -15 to 15
- projectors: bfloat16 [2, 3, 256, 256, 256], P(None, None, 'gx', 'gy'), may hold values from -6 to 6
- coupling: float32 [2, 3, 3], replicated, may hold values from -6 to 6
- positions: float32 [3, 64], replicated, may hold values from 0 to 1
- species: int32 [64], replicated, may hold values from 0 to 1
Outputs:
- hpsi: float32 [8, 256, 256, 256], P('band', 'gx', 'gy'), parts along dimension 0
There are 4 independent parts, one for each index of `band`. A program takes and returns all parts, laid end to end along the dimension named above; an argument that names none is the same for every part. Nothing has to cross between parts.
Inputs may be any that keep to these rules, and one draw needn't show every extreme that they name: species indices lie below 2.
All inputs are finite; a program needn't handle non-finite values.
Results may differ from a plain program's by a relative error of at most 0.00045.
Values sent between devices are 32-bit elements; how exact they have to be, the bound alone decides.
A program may use at most 64 MiB of HBM per device.

v0:
```python
import math

import jax
import jax.numpy as jnp
from jax import lax
from jax.sharding import PartitionSpec as P

TWO_PI = 2.0 * math.pi
HIGHEST = lax.Precision.HIGHEST


def signed_freq(index, count):
    return jnp.where(index < count // 2, index, index - count)


def axis_phase(freqs, coords):
    product = coords[:, None] * freqs[None, :].astype(jnp.float32)
    fraction = product - jnp.floor(product)
    angles = TWO_PI * fraction
    return (jnp.cos(angles), jnp.sin(angles))


def complex_einsum(einsum_form, left, right):
    left_re, left_im = left
    right_re, right_im = right

    def contract(first, second):
        return jnp.einsum(einsum_form, first, second, precision=HIGHEST)

    return (
        contract(left_re, right_re) - contract(left_im, right_im),
        contract(left_re, right_im) + contract(left_im, right_re),
    )


def conjugate(pair):
    return (pair[0], -pair[1])


def twiddle(row_index, col_index, length, phase_sign):
    turn_count = row_index[:, None] * col_index[None, :] % length
    angles = TWO_PI / length * turn_count.astype(jnp.float32)
    norm_scale = 1.0 / math.sqrt(length)
    return (jnp.cos(angles) * norm_scale, phase_sign * jnp.sin(angles) * norm_scale)


def stored_freqs(total, devices):
    row = jnp.arange(total, dtype=jnp.int32)
    block = total // devices
    return row // block + row % block * devices


def per_device(psi_coeff, potential, projectors, coupling, positions, species):
    count_x = lax.axis_size("gx")
    count_y = lax.axis_size("gy")
    rows_x, rows_y, z_length = psi_coeff.shape[1:]
    full_x = rows_x * count_x
    full_y = rows_y * count_y
    index_x = lax.axis_index("gx") + jnp.arange(rows_x, dtype=jnp.int32) * count_x
    index_y = lax.axis_index("gy") + jnp.arange(rows_y, dtype=jnp.int32) * count_y
    index_z = jnp.arange(z_length, dtype=jnp.int32)
    freq_x = signed_freq(index_x, full_x)
    freq_y = signed_freq(index_y, full_y)
    freq_z = signed_freq(index_z, z_length)
    squared = (
        (freq_x * freq_x)[:, None, None]
        + (freq_y * freq_y)[None, :, None]
        + (freq_z * freq_z)[None, None, :]
    )
    radius = min(full_x, full_y, z_length) // 4
    inside = squared <= radius * radius
    real_in = jnp.where(inside, psi_coeff[0], 0.0)
    imag_in = jnp.where(inside, psi_coeff[1], 0.0)
    all_x = jnp.arange(full_x, dtype=jnp.int32)
    all_y = jnp.arange(full_y, dtype=jnp.int32)
    order_x = stored_freqs(full_x, count_x)
    order_y = stored_freqs(full_y, count_y)
    inv_z = twiddle(index_z, index_z, z_length, 1.0)
    lines_re, lines_im = complex_einsum("hgk,kz->zgh", (real_in, imag_in), inv_z)
    lines_re, lines_im = (
        lax.all_to_all(lines_re, "gx", split_axis=0, concat_axis=2, tiled=True),
        lax.all_to_all(lines_im, "gx", split_axis=0, concat_axis=2, tiled=True),
    )
    mixed = complex_einsum(
        "zgh,hx->zgx", (lines_re, lines_im), twiddle(order_x, all_x, full_x, 1.0)
    )
    mixed_re, mixed_im = (
        lax.all_to_all(mixed[0], "gy", split_axis=0, concat_axis=1, tiled=True),
        lax.all_to_all(mixed[1], "gy", split_axis=0, concat_axis=1, tiled=True),
    )
    space_re, space_im = complex_einsum(
        "zgx,gy->zxy", (mixed_re, mixed_im), twiddle(order_y, all_y, full_y, 1.0)
    )
    field_re = potential * space_re
    field_im = potential * space_im
    fwd_z = twiddle(index_z, index_z, z_length, -1.0)
    back_re, back_im = complex_einsum(
        "zxy,yg->zgx", (field_re, field_im), twiddle(all_y, order_y, full_y, -1.0)
    )
    back_re, back_im = (
        lax.all_to_all(back_re, "gy", split_axis=1, concat_axis=0, tiled=True),
        lax.all_to_all(back_im, "gy", split_axis=1, concat_axis=0, tiled=True),
    )
    freq_re, freq_im = complex_einsum(
        "zgx,xh->zgh", (back_re, back_im), twiddle(all_x, order_x, full_x, -1.0)
    )
    freq_re, freq_im = (
        lax.all_to_all(freq_re, "gx", split_axis=2, concat_axis=0, tiled=True),
        lax.all_to_all(freq_im, "gx", split_axis=2, concat_axis=0, tiled=True),
    )
    recip_re, recip_im = complex_einsum("zgh,zk->hgk", (freq_re, freq_im), fwd_z)
    species_count = projectors.shape[0]
    atom_count = species.shape[0]
    proj_count = projectors.shape[1]
    species_table = (
        species[:, None] == jnp.arange(species_count, dtype=jnp.int32)[None, :]
    ).astype(jnp.float32)
    phase_x = axis_phase(freq_x, positions[0])
    phase_y = axis_phase(freq_y, positions[1])
    phase_z = axis_phase(freq_z, positions[2])
    weighted = (projectors * real_in, projectors * imag_in)
    along_z = complex_einsum("sqxyz,az->asqxy", weighted, phase_z)
    along_y = complex_einsum("asqxy,ay->asqx", along_z, phase_y)
    along_x = complex_einsum("asqx,ax->asq", along_y, phase_x)
    proj_norm = 4.0 / math.sqrt(full_x * full_y * z_length)
    part_re = jnp.einsum("as,asq->aq", species_table, along_x[0], precision=HIGHEST) * proj_norm
    part_im = jnp.einsum("as,asq->aq", species_table, along_x[1], precision=HIGHEST) * proj_norm
    proj_re, proj_im = lax.psum((part_re, part_im), ("gx", "gy"))
    weight_re = jnp.einsum("as,sqm,am->aq", species_table, coupling, proj_re, precision=HIGHEST)
    weight_im = jnp.einsum("as,sqm,am->aq", species_table, coupling, proj_im, precision=HIGHEST)
    back_scale = 1.0 / math.sqrt(atom_count * proj_count)
    spread_re = species_table[:, :, None] * weight_re[:, None, :] * back_scale
    spread_im = species_table[:, :, None] * weight_im[:, None, :] * back_scale
    back_x = complex_einsum("asq,ax->asqx", (spread_re, spread_im), conjugate(phase_x))
    back_y = complex_einsum("asqx,ay->asqxy", back_x, conjugate(phase_y))
    back_z = complex_einsum("asqxy,az->sqxyz", back_y, conjugate(phase_z))
    projector_re = jnp.sum(projectors * back_z[0], axis=(0, 1))
    projector_im = jnp.sum(projectors * back_z[1], axis=(0, 1))
    kinetic = squared.astype(jnp.float32) / float(radius * radius)
    out_re = jnp.where(inside, kinetic * real_in + recip_re + projector_re, 0.0)
    out_im = jnp.where(inside, kinetic * imag_in + recip_im + projector_im, 0.0)
    return jnp.stack((out_re, out_im))


def solution(mesh):
    in_specs = (
        P("band", "gx", "gy", None),
        P(("gx", "gy"), None, None),
        P(None, None, "gx", "gy", None),
        P(),
        P(),
        P(),
    )
    out_specs = P("band", "gx", "gy", None)
    return jax.shard_map(
        per_device, mesh=mesh, in_specs=in_specs, out_specs=out_specs, check_vma=False
    )
```

profile of v0, /device:TPU:24, one launch (start us, length us, event | category | flops | bytes accessed | tf_op | source)
XLA Modules:
  0.0 548.5 jit_solution(3606455159172522449)
XLA Ops:
  4.7 2.5 copy.51
  7.2 3.1 reshape.251
  10.3 15.2 %all-to-all-start = ((f32[16,1,8192]{2,1,0:T(1,128)}), f32[16,1,8192]{2,1,0:T(1,128)S(1)}, u32[]{:S(2)}, u32[]{:S(2)}) async-start(f32[16,1,8192]{2,1,0:T(1,128)} %reshape.251), calls=%async_computation | async-start | bytes 1048576 | tf_op jit(solution)/shard_map/all_to_all | solution.py:81
  28.7 2.5 copy.54
  31.1 3.2 reshape.253
  35.1 19.5 %all-to-all-done = f32[16,1,8192]{2,1,0:T(1,128)S(1)} async-done(((f32[16,1,8192]{2,1,0:T(1,128)}), f32[16,1,8192]{2,1,0:T(1,128)S(1)}, u32[]{:S(2)}, u32[]{:S(2)}) %all-to-all-start) | async-done | bytes 524320 | tf_op jit(solution)/shard_map/all_to_all | solution.py:81
  54.6 6.5 %all-to-all-start.1 = ((f32[16,1,8192]{2,1,0:T(1,128)}), f32[16,1,8192]{2,1,0:T(1,128)}, u32[]{:S(2)}, u32[]{:S(2)}) async-start(f32[16,1,8192]{2,1,0:T(1,128)} %reshape.253), calls=%async_computation.1 | async-start | bytes 1048576 | tf_op jit(solution)/shard_map/all_to_all | solution.py:82
  61.6 2.9 fusion
  64.5 3.2 fusion.1
  67.6 3.2 fusion.13
  70.8 3.7 multiply_reduce_fusion.1
  78.9 2.9 reduce.12
  81.8 2.0 reshape.252
  83.8 3.1 copy.52
  86.9 3.1 all-to-all-done.1
  90.1 2.9 reduce.13
  93.0 2.0 reshape.254
  97.2 4.3 fusion.88
  101.5 5.1 convolution_subtract_fusion
  106.7 4.7 all-to-all-start.2
  111.4 6.1 %fusion.84 = f32[16,32,256]{2,1,0:T(8,128)S(1)} fusion(f32[16,32,256]{1,2,0:T(8,128)} %bitcast.222, s32[256]{0:T(256)} %fusion.244), kind=kOutput, calls=%fused_computation.126 | convolution fusion | flops 403636224 | bytes 1049600 | tf_op jit(solution)/shard_map/zgh,hx->zgx/dot_general | solution.py:28
  117.5 5.1 convolution_add_fusion
  122.6 5.0 all-to-all-start.3
  127.7 3.4 fusion.78
  131.1 3.4 fusion.82
  134.5 3.4 all-to-all-done.3
  139.1 3.1 fusion.26
  145.0 2.0 fusion.94
  147.0 2.0 fusion.25
  150.6 4.1 all-to-all-start.4
  154.7 3.0 fusion.75
  157.8 2.6 fusion.24
  161.7 3.4 all-to-all-done.4
  165.1 4.1 all-to-all-start.5
  169.3 7.6 %fusion.174 = f32[64,1,2,3]{3,1,2,0:T(1,128)} fusion(f32[64,16,1,1]{1,2,3,0:T(1,128)S(1)} %copy.125, f32[64,2,3,16]{3,2,1,0:T(4,128)S(1)} %copy-done.5, f32[64,2,3,16]{3,2,1,0:T(4,128)S(1)} %copy-done.6), kind=kOutput, calls=%fused_computation.201 | convolution fusion | flops 79872 | bytes 54784 | tf_op jit(solution)/shard_map/asqx,ax->asq/dot_general | solution.py:28
  176.9 7.6 %fusion.176 = f32[64,1,2,3]{3,1,2,0:T(1,128)} fusion(f32[64,16,1,1]{1,2,3,0:T(1,128)S(1)} %copy.111, f32[64,2,3,16]{3,2,1,0:T(4,128)S(1)} %copy-done.5, f32[64,2,3,16]{3,2,1,0:T(4,128)S(1)} %copy-done.6), kind=kOutput, calls=%fused_computation.203 | convolution fusion | flops 79872 | bytes 54784 | tf_op jit(solution)/shard_map/asqx,ax->asq/dot_general | solution.py:28
  187.5 2.6 fusion.73
  190.1 3.0 convolution_subtract_fusion.2
  193.2 3.5 copy.73
  196.7 3.1 reshape.255
  199.8 9.1 %all-to-all-start.6 = ((f32[16,1,8192]{2,1,0:T(1,128)}), f32[16,1,8192]{2,1,0:T(1,128)}, u32[]{:S(2)}, u32[]{:S(2)}) async-start(f32[16,1,8192]{2,1,0:T(1,128)} %reshape.255), calls=%async_computation.6 | async-start | bytes 1048576 | tf_op jit(solution)/shard_map/all_to_all | solution.py:108
  208.8 7.9 %fusion.170 = f32[64,1,2,3]{3,1,2,0:T(1,128)S(1)} fusion(f32[64,16,1,1]{1,2,3,0:T(1,128)S(1)} %copy.111, f32[64,2,3,16]{3,2,1,0:T(4,128)S(1)} %copy.118, f32[64,2,3,16]{3,2,1,0:T(4,128)} %copy.124), kind=kOutput, calls=%fused_computation.197 | convolution fusion | flops 79872 | bytes 54784 | tf_op jit(solution)/shard_map/asqx,ax->asq/dot_general | solution.py:28
  216.8 8.0 %fusion.172 = f32[64,1,2,3]{3,1,2,0:T(1,128)S(1)} fusion(f32[64,16,1,1]{1,2,3,0:T(1,128)S(1)} %copy.125, f32[64,2,3,16]{3,2,1,0:T(4,128)S(1)} %copy.118, f32[64,2,3,16]{3,2,1,0:T(4,128)} %copy.124), kind=kOutput, calls=%fused_computation.199 | convolution fusion | flops 79872 | bytes 54784 | tf_op jit(solution)/shard_map/asqx,ax->asq/dot_general | solution.py:28
  226.0 252.1 %all-reduce = (f32[64,3]{0,1:T(4,128)S(1)}, f32[64,3]{0,1:T(4,128)S(1)}) all-reduce(f32[64,3]{0,1:T(4,128)S(1)} %broadcast_multiply_fusion, f32[64,3]{0,1:T(4,128)S(1)} %broadcast_multiply_fusion.1), channel_id=1, replica_groups=mesh['band'=4,'gx'=16,'gy'=8] {'gx','gy'}, use_global_device_ids=true, to_apply=%region_1.2 | all-reduce | flops 384 | bytes 3072 | tf_op jit(solution)/shard_map/psum | solution.py:128
  480.4 2.6 fusion.69
  483.0 3.0 convolution_add_fusion.2
  486.0 3.5 copy.77
  489.5 3.1 reshape.257
  492.6 10.4 %all-to-all-start.7 = ((f32[16,1,8192]{2,1,0:T(1,128)}), f32[16,1,8192]{2,1,0:T(1,128)}, u32[]{:S(2)}, u32[]{:S(2)}) async-start(f32[16,1,8192]{2,1,0:T(1,128)} %reshape.257), calls=%async_computation.7 | async-start | bytes 1048576 | tf_op jit(solution)/shard_map/all_to_all | solution.py:109
  503.1 2.9 fusion.6
  506.0 2.9 fusion.7
  508.9 3.8 fusion.5
  512.7 3.0 fusion.4
  515.7 3.1 reduce.14
  518.8 2.0 reshape.256
  520.8 3.6 copy.75
  524.4 2.5 copy.76
  526.9 2.4 fusion.66
  529.3 2.4 fusion.97
  531.7 2.9 reduce.15
  534.6 2.0 reshape.258
  536.6 3.6 copy.79
  540.2 2.6 copy.80
  542.8 2.8 fusion.18
  (97 shorter events, 31.7 us)
Async XLA Ops:
  0.0 478.1 %copy-start = (f32[2,3,3]{2,0,1:T(2,128)S(1)}, f32[2,3,3]{2,0,1:T(2,128)}, u32[]{:S(2)}) copy-start(f32[2,3,3]{2,0,1:T(2,128)} %param.9) | copy-start | bytes 220
  0.0 3.1 copy-start.21
  10.3 44.3 %all-to-all-start = ((f32[16,1,8192]{2,1,0:T(1,128)}), f32[16,1,8192]{2,1,0:T(1,128)S(1)}, u32[]{:S(2)}, u32[]{:S(2)}) async-start(f32[16,1,8192]{2,1,0:T(1,128)} %reshape.251), calls=%async_computation | async-start | bytes 1048576 | tf_op jit(solution)/shard_map/all_to_all | solution.py:81
  31.1 3.2 copy-start.23
  31.1 30.0 %copy-start.24 = (s32[64]{0:T(128)S(1)}, s32[64]{0:T(128)}, u32[]{:S(2)}) copy-start(s32[64]{0:T(128)} %param.11) | copy-start | bytes 772
  31.1 30.4 %copy-start.1 = (bf16[2,3,16,32,256]{4,3,2,1,0:T(8,128)(2,1)S(1)}, bf16[2,3,16,32,256]{4,3,2,1,0:T(8,128)(2,1)}, u32[]{:S(2)}) copy-start(bf16[2,3,16,32,256]{4,3,2,1,0:T(8,128)(2,1)} %param.8) | copy-start | bytes 4718596
  34.4 36.4 %copy-start.13 = (f32[64]{0:T(128)}, f32[64]{0:T(128)S(1)}, u32[]{:S(2)}) copy-start(f32[64]{0:T(128)S(1)} %get-tuple-element.19) | copy-start | bytes 772
  54.6 9.9 %copy-start.8 = (f32[16,1,8192]{2,1,0:T(1,128)}, f32[16,1,8192]{2,1,0:T(1,128)S(1)}, u32[]{:S(2)}) copy-start(f32[16,1,8192]{2,1,0:T(1,128)S(1)} %all-to-all-done) | copy-start | bytes 1572868
  54.6 35.5 %all-to-all-start.1 = ((f32[16,1,8192]{2,1,0:T(1,128)}), f32[16,1,8192]{2,1,0:T(1,128)}, u32[]{:S(2)}, u32[]{:S(2)}) async-start(f32[16,1,8192]{2,1,0:T(1,128)} %reshape.253), calls=%async_computation.1 | async-start | bytes 1048576 | tf_op jit(solution)/shard_map/all_to_all | solution.py:82
  61.1 3.3 copy-start.19
  95.0 2.2 copy-start.2
  95.0 2.2 copy-start.15
  96.9 4.6 copy-start.3
  106.7 16.0 %all-to-all-start.2 = ((f32[16,32,256]{2,1,0:T(8,128)}), f32[16,32,256]{2,1,0:T(8,128)S(1)}, u32[]{:S(2)}, u32[]{:S(2)}) async-start(f32[16,32,256]{2,1,0:T(8,128)} %convolution_subtract_fusion), calls=%async_computation.2 | async-start | bytes 1048576 | tf_op jit(solution)/shard_map/all_to_all | solution.py:88
  111.4 6.1 %copy-start.4 = (f32[16,32,16,16]{1,3,2,0:T(8,128)S(1)}, f32[16,32,16,16]{1,3,2,0:T(8,128)}, u32[]{:S(2)}) copy-start(f32[16,32,16,16]{1,3,2,0:T(8,128)} %copy-done.3) | copy-start | bytes 1572868
  111.4 6.1 %copy-start.16 = (s32[256]{0:T(256)S(1)}, s32[256]{0:T(256)}, u32[]{:S(2)}) copy-start(s32[256]{0:T(256)} %fusion.244) | copy-start | bytes 3076
  122.6 15.3 %all-to-all-start.3 = ((f32[16,32,256]{2,1,0:T(8,128)}), f32[16,32,256]{2,1,0:T(8,128)}, u32[]{:S(2)}, u32[]{:S(2)}) async-start(f32[16,32,256]{2,1,0:T(8,128)} %convolution_add_fusion), calls=%async_computation.3 | async-start | bytes 1048576 | tf_op jit(solution)/shard_map/all_to_all | solution.py:89
  137.9 4.3 copy-start.9
  137.9 4.3 copy-start.12
  137.9 4.3 copy-start.20
  144.2 0.8 copy-start.11
  150.6 14.5 %all-to-all-start.4 = ((f32[2,256,256]{2,0,1:T(2,128)}), f32[2,256,256]{2,0,1:T(2,128)}, u32[]{:S(2)}, u32[]{:S(2)}) async-start(f32[2,256,256]{2,0,1:T(2,128)} %copy.67), calls=%async_computation.4 | async-start | bytes 1048576 | tf_op jit(solution)/shard_map/all_to_all | solution.py:101
  160.4 8.8 %copy-start.5 = (f32[64,2,3,16]{3,2,1,0:T(4,128)S(1)}, f32[64,2,3,16]{3,2,1,0:T(4,128)}, u32[]{:S(2)}) copy-start(f32[64,2,3,16]{3,2,1,0:T(4,128)} %copy.104) | copy-start | bytes 73732
  160.4 8.8 %copy-start.6 = (f32[64,2,3,16]{3,2,1,0:T(4,128)S(1)}, f32[64,2,3,16]{3,2,1,0:T(4,128)}, u32[]{:S(2)}) copy-start(f32[64,2,3,16]{3,2,1,0:T(4,128)} %copy.110) | copy-start | bytes 73732
  165.1 21.3 %all-to-all-start.5 = ((f32[2,256,256]{2,0,1:T(2,128)}), f32[2,256,256]{2,0,1:T(2,128)}, u32[]{:S(2)}, u32[]{:S(2)}) async-start(f32[2,256,256]{2,0,1:T(2,128)} %copy.71), calls=%async_computation.5 | async-start | bytes 1048576 | tf_op jit(solution)/shard_map/all_to_all | solution.py:102
  199.8 292.9 %all-to-all-start.6 = ((f32[16,1,8192]{2,1,0:T(1,128)}), f32[16,1,8192]{2,1,0:T(1,128)}, u32[]{:S(2)}, u32[]{:S(2)}) async-start(f32[16,1,8192]{2,1,0:T(1,128)} %reshape.255), calls=%async_computation.6 | async-start | bytes 1048576 | tf_op jit(solution)/shard_map/all_to_all | solution.py:108
  489.5 13.6 %copy-start.17 = (f32[64,16]{0,1:T(8,128)S(1)}, f32[64,16]{0,1:T(8,128)}, u32[]{:S(2)}) copy-start(f32[64,16]{0,1:T(8,128)} %get-tuple-element.24) | copy-start | bytes 12292
  489.5 13.6 %copy-start.18 = (f32[64,16]{0,1:T(8,128)S(1)}, f32[64,16]{0,1:T(8,128)}, u32[]{:S(2)}) copy-start(f32[64,16]{0,1:T(8,128)} %get-tuple-element.27) | copy-start | bytes 12292
  489.5 13.6 %copy-start.14 = (f32[64]{0:T(128)S(1)}, f32[64]{0:T(128)}, u32[]{:S(2)}) copy-start(f32[64]{0:T(128)} %copy-done.13) | copy-start | bytes 772
  492.6 39.1 %all-to-all-start.7 = ((f32[16,1,8192]{2,1,0:T(1,128)}), f32[16,1,8192]{2,1,0:T(1,128)}, u32[]{:S(2)}, u32[]{:S(2)}) async-start(f32[16,1,8192]{2,1,0:T(1,128)} %reshape.257), calls=%async_computation.7 | async-start | bytes 1048576 | tf_op jit(solution)/shard_map/all_to_all | solution.py:109
  540.2 2.6 copy-start.7
  540.2 2.6 copy-start.22
  542.7 2.8 copy-start.10
where the time goes:
time: 558 us; the launch traced here: 549 us
  blocking collectives  252 us (45%)
  matrix products  127 us (23%)
  local copies, waits for them, and re-layouts  61.5 us (11%)
  starting transfers between devices  59.2 us (11%)
  waiting for transfers between devices  29.4 us (5%)
  other arithmetic  18.1 us (3%)
    psum x1, blocking collectives, per_device(): proj_re, proj_im = lax.psum((part_re, part_im), ('gx', 'gy'))  252 us
    dot_general x36, matrix products, contract(): return jnp.einsum(einsum_form, first, second, precision=HIGHEST)  126 us
    unnamed x59, local copies, waits for them, and re-layouts  21.8 us
    all_to_all x1, waiting for transfers between devices, per_device(): lax.all_to_all(lines_re, 'gx', split_axis=0, concat_axis=2, tiled=True)  19.5 us
    all_to_all x1, starting transfers between devices, per_device(): lax.all_to_all(lines_re, 'gx', split_axis=0, concat_axis=2, tiled=True)  15.2 us
  transfers between devices with their start and end apart: 8, of which 4 were waited for; matrix products, arithmetic and copies ran while one was open for 25% of the time, Pallas kernels for 0%

commit v1 on v0

v1 whole, which is shorter than its diff:
```python
import functools
import math

import jax
import jax.numpy as jnp
import ml_dtypes
import numpy as np
from jax import lax
from jax.experimental import pallas as pl
from jax.experimental.pallas import tpu as pltpu
from jax.sharding import PartitionSpec as P

MESH = pl.DeviceIdType.MESH
N = 256
GX = 16
GY = 8
COLS = 128
RADIUS = 64
ATOMS = 64
NSPEC = 2
LPROJ = 3
TWO_PI = 2.0 * math.pi
ROWS_X = (0, 1, 2, 3, 12, 13, 14, 15)
HELD_X = (0, 1, 2, 3, 5, 6, 7, 8)
COL_Y = 71
COL_X = 72


def column_offsets(col):
    a = col // 16
    b = col % 16
    a = a - 8 * (a >= 4)
    b = b - 16 * (b >= 8)
    a = np.where(col == COL_Y, 0, np.where(col == COL_X, 4, a))
    b = np.where(col == COL_Y, 8, np.where(col == COL_X, 0, b))
    return a, b


def two_parts(table):
    table = table.astype(np.float32)
    high = table.astype(ml_dtypes.bfloat16)
    low = (table - high.astype(np.float32)).astype(ml_dtypes.bfloat16)
    return np.stack([high, low])


@functools.lru_cache(maxsize=None)
def tables():
    t, g, c, y = np.meshgrid(
        np.arange(2), np.arange(GX), np.arange(2), np.arange(GY), indexing="ij"
    )
    z = (16 * g + 2 * y + t).reshape(-1, 1)
    c = c.reshape(-1, 1)
    angle = TWO_PI / N * (z * np.arange(N)[None, :] % N)
    cos, sin = np.cos(angle) / 16, np.sin(angle) / 16
    tz = np.concatenate(
        [np.where(c == 0, cos, sin), np.where(c == 0, -sin, cos)], axis=1
    )
    a, b = column_offsets(np.arange(COLS))
    x0 = np.repeat(np.arange(16), 32)[None, :]
    y0 = np.tile(np.arange(32), 16)[None, :]
    angle = TWO_PI * ((2 * a[:, None] * x0 + b[:, None] * y0) % 32) / 32
    cos, sin = np.cos(angle) / 16, np.sin(angle) / 16
    t1 = np.block([[cos, sin], [-sin, cos]])
    gy = np.repeat(np.arange(GY), GX)[:, None]
    gx = np.tile(np.arange(GX), GY)[:, None]
    angle = TWO_PI * ((gx * x0 + gy * y0) % N) / N
    t2 = np.stack([np.cos(angle), np.sin(angle)]).astype(np.float32)
    y1, x1 = gy, gx
    angle = TWO_PI * ((gx.T * x1 + 2 * gy.T * y1) % 16) / 16
    cos, sin = np.cos(angle) / 16, np.sin(angle) / 16
    e = np.block([[cos, -sin], [sin, cos]])
    return (
        two_parts(tz),
        two_parts(t1),
        two_parts(t1.T),
        np.concatenate([two_parts(e), two_parts(e.T)]),
        t2,
    )


def split(value):
    high = value.astype(jnp.bfloat16)
    return high, (value - high.astype(jnp.float32)).astype(jnp.bfloat16)


def product(left, right, dims=((1,), (0,))):
    def one(first, second):
        return lax.dot_general(
            first, second, (dims, ((), ())), preferred_element_type=jnp.float32
        )

    return one(left[0], right[0]) + (one(left[0], right[1]) + one(left[1], right[0]))


def cos_turns(turns):
    r = (turns - jnp.floor(turns + 0.5)) * math.pi
    r2 = r * r
    s = -1.0 / 39916800.0
    for denom in (362880.0, -5040.0, 120.0, -6.0, 1.0):
        s = s * r2 + 1.0 / denom
    s = s * r
    return 1.0 - 2.0 * s * s


def iota(shape, axis):
    return lax.broadcasted_iota(jnp.int32, shape, axis)


def column_freqs(gx, gy, shape):
    col = iota(shape, 0)
    a = lax.shift_right_logical(col, 4)
    b = col & 15
    a = jnp.where(a >= 4, a - 8, a)
    b = jnp.where(b >= 8, b - 16, b)
    a = jnp.where(col == COL_Y, 0, jnp.where(col == COL_X, 4, a))
    b = jnp.where(col == COL_Y, 8, jnp.where(col == COL_X, 0, b))
    return gx + GX * a, gy + GY * b


def fractional(product_):
    return product_ - jnp.floor(product_)


def pick_columns(held):
    tiles = []
    for place, i in enumerate(HELD_X):
        row = held(i)
        first, second = row[0:8], row[24:32]
        if place == 4:
            sub = iota((8, N), 0)
            other = jnp.broadcast_to(held(0)[8:9], (8, N))
            first = jnp.where(sub == 7, other, first)
            other = jnp.broadcast_to(held(4)[0:1], (8, N))
            second = jnp.where(sub == 0, other, second)
        tiles += [first, second]
    return jnp.concatenate(tiles, axis=0)


def kernel(
    psi_h, pot_h, proj_h, coup, pos, spec, tz_h, t1_h, t1t_h, e_h, t2_h,
    out,
    psi, pot, proj, tz, t1, t1t, e, t2,
    xs, pf, pz, pxy, vt, nl,
    zs, r1, s2, r2, s3, r3, s4, r4, ar0, ar1, ar2,
    load_sem, sx, rx, sy, ry,
):
    gx = lax.axis_index("gx")
    gy = lax.axis_index("gy")
    loads = []
    pairs = [
        (psi_h.at[:, 0:5], psi.at[:, 0:5]),
        (psi_h.at[:, 12:16], psi.at[:, 5:9]),
        (tz_h, tz),
        (proj_h.at[:, :, 0:5], proj.at[:, :, 0:5]),
        (proj_h.at[:, :, 12:16], proj.at[:, :, 5:9]),
        (pot_h.at[:, :, 0:128], pot.at[0]),
        (pot_h.at[:, :, 128:256], pot.at[1]),
        (t1_h, t1),
        (t2_h, t2),
        (e_h, e),
        (t1t_h, t1t),
    ]
    for i, (src, dst) in enumerate(pairs):
        loads.append(pltpu.make_async_copy(src, dst, load_sem.at[i]))
        loads[-1].start()

    barrier = pltpu.get_barrier_semaphore()

    @pl.loop(1, GX)
    def _(d):
        pl.semaphore_signal(
            barrier, inc=1, device_id={"gx": lax.rem(gx + d, GX)}, device_id_type=MESH
        )

    @pl.loop(1, GY)
    def _(d):
        pl.semaphore_signal(
            barrier, inc=1, device_id={"gy": lax.rem(gy + d, GY)}, device_id_type=MESH
        )

    def over_x(slot, d, source, target):
        peer = lax.rem(gx + d, GX)
        return pltpu.make_async_remote_copy(
            src_ref=source(peer),
            dst_ref=target(gx),
            send_sem=sx.at[slot, d],
            recv_sem=rx.at[slot, d],
            device_id={"gx": peer},
            device_id_type=MESH,
        )

    def over_y(slot, d, source, target):
        peer = lax.rem(gy + d, GY)
        return pltpu.make_async_remote_copy(
            src_ref=source(peer),
            dst_ref=target(gy),
            send_sem=sy.at[slot, d],
            recv_sem=ry.at[slot, d],
            device_id={"gy": peer},
            device_id_type=MESH,
        )

    def send(over, count, slot, source, target):
        @pl.loop(1, count)
        def _(d):
            over(slot, d, source, target).start()

    def receive(over, count, slot, source, target):
        @pl.loop(1, count)
        def _(d):
            over(slot, d, source, target).wait()

    def rows16(i):
        return pl.ds(pl.multiple_of(i * 16, 16), 16)

    def rows32(i):
        return pl.ds(pl.multiple_of(i * 32, 32), 32)

    kx, ky = column_freqs(gx, gy, (COLS, N))
    lane = iota((COLS, N), 1)
    kz = jnp.where(lane < N // 2, lane, lane - N)
    squared = kx * kx + ky * ky + kz * kz
    inside = squared <= RADIUS * RADIUS
    kinetic = squared.astype(jnp.float32) * (1.0 / (RADIUS * RADIUS))
    loads[0].wait()
    loads[1].wait()
    for c in range(2):
        xs[c] = jnp.where(inside, pick_columns(lambda i: psi[c, i]), 0.0)
    x_parts = split(jnp.concatenate([xs[0], xs[1]], axis=1))
    loads[2].wait()

    def tz_parts(t):
        rows = pl.ds(256 * t, 256)
        return tz[0, rows, :], tz[1, rows, :]

    p1 = [(lambda p, t=t: zs.at[t, p], lambda m, t=t: r1.at[t, rows16(m)]) for t in range(2)]
    p2 = [(lambda p, t=t: s2.at[t, p], lambda m, t=t: r2.at[t, m]) for t in range(2)]
    p3 = [(lambda p, t=t: s3.at[t, p], lambda m, t=t: r3.at[t, rows32(m)]) for t in range(2)]
    p4 = [(lambda p, t=t: s4.at[t, p], lambda m, t=t: r4.at[t, m]) for t in range(2)]

    for t in range(2):
        lines = product(tz_parts(t), x_parts, ((1,), (1,)))
        zs[t] = lines.reshape(GX, 16, COLS)
        if t == 0:
            pl.semaphore_wait(barrier, GX + GY - 2)
        send(over_x, GX, t, *p1[t])
        r1[t, rows16(gx), :] = zs[t, gx]

    atoms2 = jnp.concatenate([pos[...], pos[...]], axis=1)
    half = iota((1, 2 * ATOMS), 1) >= ATOMS
    quarter = jnp.where(half, 0.25, 0.0)
    row = iota((N, 2 * ATOMS), 0)
    kz_rows = jnp.where(row < N // 2, row, row - N).astype(jnp.float32)
    turns_z = fractional(kz_rows * atoms2[2:3])
    pz_f32 = jnp.concatenate(
        [cos_turns(turns_z - quarter), cos_turns(turns_z + (0.25 - quarter))], axis=0
    )
    pz[0], pz[1] = split(pz_f32)
    kx_col, ky_col = column_freqs(gx, gy, (COLS, 2 * ATOMS))
    turns_xy = fractional(kx_col.astype(jnp.float32) * atoms2[0:1]) + fractional(
        ky_col.astype(jnp.float32) * atoms2[1:2]
    )
    pxy[0] = cos_turns(turns_xy)
    pxy[1] = cos_turns(turns_xy + jnp.where(half, -0.25, 0.25))

    loads[3].wait()
    loads[4].wait()
    pz_parts = (pz[0], pz[1])
    sums = []
    for s in range(NSPEC):
        for q in range(LPROJ):
            factor = pick_columns(lambda i: proj[s, q, i].astype(jnp.float32))
            pf[s * LPROJ + q] = factor
            weighted = jnp.concatenate([factor * xs[0], factor * xs[1]], axis=1)
            along_z = product(split(weighted), pz_parts)
            along = along_z * pxy[0] + pltpu.roll(along_z, ATOMS, 1) * pxy[1]
            sums.append(jnp.sum(along, axis=0, keepdims=True))
    species = jnp.concatenate([spec[...], spec[...]], axis=1)
    norm = 4.0 / math.sqrt(N * N * N)
    sub = iota((8, 2 * ATOMS), 0)
    part = jnp.zeros((8, 2 * ATOMS), jnp.float32)
    for q in range(LPROJ):
        chosen = jnp.where(species == 0, sums[q], sums[LPROJ + q]) * norm
        part = jnp.where(sub == q, chosen, part)
    ar0[0] = part
    ar1[gx] = part
    a1 = (lambda p: ar0.at[0], lambda m: ar1.at[m])
    a2 = (lambda p: ar0.at[1], lambda m: ar2.at[m])
    send(over_x, GX, 4, *a1)

    loads[5].wait()
    loads[6].wait()
    lane16 = iota((16, 128), 1)
    for t in range(2):
        for block in range(4):
            for hy in range(2):
                strips = [
                    pot[hy, t, pl.ds(4 * block + j, 16, stride=16), :] for j in range(4)
                ]
                for r in range(4):
                    tile = None
                    for j in range(4):
                        shift = (32 * (j - r)) % 128
                        moved = strips[j] if shift == 0 else pltpu.roll(strips[j], shift, 1)
                        tile = moved if tile is None else jnp.where(lane16 >= 32 * j, moved, tile)
                    y1 = 4 * hy + r
                    vt[t, pl.ds(16 * y1, 16), pl.ds(128 * block, 128)] = tile

    def pass_on(t):
        receive(over_x, GX, t, *p1[t])
        for g in range(GY):
            for c in range(2):
                s2[t, g, pl.ds(16 * c, 16), :] = r1[t, pl.ds(8 * c + g, 16, stride=16), :]
        send(over_y, GY, t, *p2[t])
        r2[t, gy] = s2[t, gy]

    def plane(t):
        receive(over_y, GY, t, *p2[t])
        values = jnp.concatenate(
            [r2[t, :, 0:16, :].reshape(COLS, COLS), r2[t, :, 16:32, :].reshape(COLS, COLS)],
            axis=1,
        )
        lanes = product(split(values), (t1[0], t1[1]))
        lanes_re, lanes_im = lanes[:, :512], lanes[:, 512:]
        cos, sin = t2[0], t2[1]
        turned = jnp.concatenate(
            [lanes_re * cos - lanes_im * sin, lanes_re * sin + lanes_im * cos], axis=0
        )
        space = product((e[0], e[1]), split(turned))
        field = jnp.concatenate([space[:128] * vt[t], space[128:] * vt[t]], axis=0)
        rows = product((e[2], e[3]), split(field))
        rows_re, rows_im = rows[:128], rows[128:]
        turned = jnp.concatenate(
            [rows_re * cos + rows_im * sin, rows_im * cos - rows_re * sin], axis=1
        )
        back = product(split(turned), (t1t[0], t1t[1]))
        s3[t, :, 0:16, :] = back[:, :128].reshape(GY, 16, COLS)
        s3[t, :, 16:32, :] = back[:, 128:].reshape(GY, 16, COLS)
        send(over_y, GY, 2 + t, *p3[t])
        r3[t, rows32(gy), :] = s3[t, gy]

    def return_on(t):
        receive(over_y, GY, 2 + t, *p3[t])
        for g in range(GX):
            for c in range(2):
                s4[t, g, pl.ds(8 * c, 8), :] = r3[t, pl.ds(16 * c + g, 8, stride=32), :]
        send(over_x, GX, 2 + t, *p4[t])
        r4[t, gx] = s4[t, gx]

    pass_on(0)
    receive(over_x, GX, 4, *a1)
    total = ar1[0]
    for g in range(1, GX):
        total += ar1[g]
    ar0[1] = total
    ar2[gy] = total
    send(over_y, GY, 4, *a2)
    for i in range(7, 11):
        loads[i].wait()
    plane(0)
    pass_on(1)
    return_on(0)
    plane(1)
    return_on(1)

    receive(over_y, GY, 4, *a2)
    total = ar2[0]
    for g in range(1, GY):
        total += ar2[g]
    spread = []
    for s in range(NSPEC):
        for q in range(LPROJ):
            weight = coup[s, q, 0] * total[0:1]
            for m in range(1, LPROJ):
                weight += coup[s, q, m] * total[m : m + 1]
            weight = weight * (1.0 / math.sqrt(ATOMS * LPROJ))
            spread.append(jnp.where(species == s, weight, 0.0))
    nonloc = None
    for i, weight in enumerate(spread):
        around = pltpu.roll(jnp.broadcast_to(weight, (8, 2 * ATOMS)), ATOMS, 1)[0:1]
        at_columns = pxy[0] * weight - pxy[1] * around
        spread_z = product(split(at_columns), pz_parts, ((1,), (1,)))
        term = jnp.concatenate([pf[i] * spread_z[:, :N], pf[i] * spread_z[:, N:]], axis=1)
        nonloc = term if nonloc is None else nonloc + term
    for c in range(2):
        nl[c] = nonloc[:, c * N : (c + 1) * N] + kinetic * xs[c]

    recip = None
    for t in range(2):
        receive(over_x, GX, 2 + t, *p4[t])
        lines = r4[t].reshape(256, COLS)
        term = product(split(jnp.transpose(lines)), tz_parts(t))
        recip = term if recip is None else recip + term
    for c in range(2):
        out[c] = jnp.where(inside, nl[c] + recip[:, c * N : (c + 1) * N], 0.0)


def place(columns, out):
    sub = iota((8, N), 0)
    for c in range(2):
        for row in range(16):
            if row in ROWS_X:
                base = 16 * ROWS_X.index(row)
                out[c, row, 0:8, :] = columns[c, base : base + 8, :]
                out[c, row, 8:24, :] = jnp.zeros((16, N), jnp.float32)
                out[c, row, 24:32, :] = columns[c, base + 8 : base + 16, :]
            else:
                out[c, row] = jnp.zeros((32, N), jnp.float32)
        along_y = jnp.broadcast_to(columns[c, COL_Y : COL_Y + 1, :], (8, N))
        out[c, 0, 8:16, :] = jnp.where(sub == 0, along_y, 0.0)
        along_x = jnp.broadcast_to(columns[c, COL_X : COL_X + 1, :], (8, N))
        out[c, 4, 0:8, :] = jnp.where(sub == 0, along_x, 0.0)
        corner = columns[c, 64:72, :]
        out[c, 12, 0:8, :] = jnp.where(sub == 7, 0.0, corner)
        corner = columns[c, 72:80, :]
        out[c, 12, 24:32, :] = jnp.where(sub == 0, 0.0, corner)


def per_device(psi_coeff, potential, projectors, coupling, positions, species):
    f32, bf16 = jnp.float32, jnp.bfloat16
    consts = [jnp.asarray(table) for table in tables()]
    hbm = pl.BlockSpec(memory_space=pl.ANY)
    vmem = pl.BlockSpec(memory_space=pltpu.VMEM)
    smem = pl.BlockSpec(memory_space=pltpu.SMEM)
    columns = pl.pallas_call(
        kernel,
        out_shape=jax.ShapeDtypeStruct((2, COLS, N), f32),
        in_specs=[hbm, hbm, hbm, smem, vmem, vmem] + [hbm] * 5,
        out_specs=vmem,
        scratch_shapes=[
            pltpu.VMEM((2, 9, 32, N), f32),
            pltpu.VMEM((2, 2, N, 128), f32),
            pltpu.VMEM((NSPEC, LPROJ, 9, 32, N), bf16),
            pltpu.VMEM((2, 512, 512), bf16),
            pltpu.VMEM((2, 256, 1024), bf16),
            pltpu.VMEM((2, 1024, 256), bf16),
            pltpu.VMEM((4, 256, 256), bf16),
            pltpu.VMEM((2, 128, 512), f32),
            pltpu.VMEM((2, COLS, N), f32),
            pltpu.VMEM((NSPEC * LPROJ, COLS, N), f32),
            pltpu.VMEM((2, 2 * N, 2 * ATOMS), bf16),
            pltpu.VMEM((2, COLS, 2 * ATOMS), f32),
            pltpu.VMEM((2, 128, 512), f32),
            pltpu.VMEM((2, COLS, N), f32),
            pltpu.VMEM((2, GX, 16, COLS), f32),
            pltpu.VMEM((2, GX * 16, COLS), f32),
            pltpu.VMEM((2, GY, 32, COLS), f32),
            pltpu.VMEM((2, GY, 32, COLS), f32),
            pltpu.VMEM((2, GY, 32, COLS), f32),
            pltpu.VMEM((2, GY * 32, COLS), f32),
            pltpu.VMEM((2, GX, 16, COLS), f32),
            pltpu.VMEM((2, GX, 16, COLS), f32),
            pltpu.VMEM((2, 8, 128), f32),
            pltpu.VMEM((GX, 8, 128), f32),
            pltpu.VMEM((GY, 8, 128), f32),
            pltpu.SemaphoreType.DMA((11,)),
            pltpu.SemaphoreType.DMA((5, GX)),
            pltpu.SemaphoreType.DMA((5, GX)),
            pltpu.SemaphoreType.DMA((5, GY)),
            pltpu.SemaphoreType.DMA((5, GY)),
        ],
        compiler_params=pltpu.CompilerParams(
            collective_id=0, has_side_effects=True, vmem_limit_bytes=48 * 1024 * 1024
        ),
    )(psi_coeff, potential, projectors, coupling, positions, species.reshape(1, ATOMS), *consts)
    return pl.pallas_call(
        place,
        out_shape=jax.ShapeDtypeStruct((2, 16, 32, N), f32),
        in_specs=[vmem],
        out_specs=vmem,
    )(columns)


def solution(mesh):
    in_specs = (
        P("band", "gx", "gy", None),
        P(("gx", "gy"), None, None),
        P(None, None, "gx", "gy", None),
        P(),
        P(),
        P(),
    )
    out_specs = P("band", "gx", "gy", None)
    return jax.shard_map(
        per_device, mesh=mesh, in_specs=in_specs, out_specs=out_specs, check_vma=False
    )
```

time: 558 us -> 76.2 us (0.14)
  the two profiles are of different devices: /device:TPU:24 before, /device:TPU:1 now
where the time goes in v1:
time: 76.2 us; the launch traced here: 75.7 us
  Pallas kernels  64.9 us (85%)
  local copies, waits for them, and re-layouts  10.7 us (14%)
    pallas_call x1, Pallas kernels, per_device(): pl.pallas_call(kernel, out_shape=jax.ShapeDtypeStruct((2, COLS, N), f32),...  62.9 us
    unnamed x21, local copies, waits for them, and re-layouts  10.7 us
    pallas_call x1, Pallas kernels, per_device(): pl.pallas_call(place, out_shape=jax.ShapeDtypeStruct((2, 16, 32, N), f32)...  1.99 us

profile of v1, /device:TPU:1, one launch (start us, length us, event | category | flops | bytes accessed | tf_op | source)
XLA Modules:
  0.0 75.7 jit_solution(2438115683750752774)
XLA Ops:
  0.0 0.7 copy.12.coup
  0.7 0.0 copy-start.1
  0.7 1.2 %copy-done.1 = f32[2,16,32,256]{3,2,1,0:T(8,128)S(1)} copy-done((f32[2,16,32,256]{3,2,1,0:T(8,128)S(1)}, f32[2,16,32,256]{3,2,1,0:T(8,128)}, u32[]{:S(2)}) %copy-start.1) | copy-done | bytes 1048600
  1.9 0.0 copy-start.2
  1.9 1.2 %copy-done.2 = bf16[2,1024,256]{2,1,0:T(8,128)(2,1)S(1)} copy-done((bf16[2,1024,256]{2,1,0:T(8,128)(2,1)S(1)}, bf16[2,1024,256]{2,1,0:T(8,128)(2,1)}, u32[]{:S(2)}) %copy-start.2) | copy-done | bytes 1048600
  3.1 0.0 copy-start.3
  3.1 1.2 %copy-done.3 = bf16[2,256,1024]{2,1,0:T(8,128)(2,1)S(1)} copy-done((bf16[2,256,1024]{2,1,0:T(8,128)(2,1)S(1)}, bf16[2,256,1024]{2,1,0:T(8,128)(2,1)}, u32[]{:S(2)}) %copy-start.3) | copy-done | bytes 1048600
  4.4 0.0 copy-start.4
  4.4 1.2 %copy-done.4 = bf16[2,512,512]{2,1,0:T(8,128)(2,1)S(1)} copy-done((bf16[2,512,512]{2,1,0:T(8,128)(2,1)S(1)}, bf16[2,512,512]{2,1,0:T(8,128)(2,1)}, u32[]{:S(2)}) %copy-start.4) | copy-done | bytes 1048600
  5.6 0.0 copy-start.5
  5.6 1.0 %copy-done.5 = f32[2,256,256]{2,1,0:T(8,128)S(1)} copy-done((f32[2,256,256]{2,1,0:T(8,128)S(1)}, f32[2,256,256]{2,1,0:T(8,128)}, u32[]{:S(2)}) %copy-start.5) | copy-done | bytes 524312
  6.6 0.0 copy-start.6
  6.6 1.0 %copy-done.6 = f32[2,128,512]{2,1,0:T(8,128)S(1)} copy-done((f32[2,128,512]{2,1,0:T(8,128)S(1)}, f32[2,128,512]{2,1,0:T(8,128)}, u32[]{:S(2)}) %copy-start.6) | copy-done | bytes 524312
  7.7 0.0 copy-start.7
  7.7 1.0 %copy-done.7 = bf16[4,256,256]{2,1,0:T(8,128)(2,1)S(1)} copy-done((bf16[4,256,256]{2,1,0:T(8,128)(2,1)S(1)}, bf16[4,256,256]{2,1,0:T(8,128)(2,1)}, u32[]{:S(2)}) %copy-start.7) | copy-done | bytes 524312
  8.7 0.0 copy-start.8
  8.7 0.7 copy-done.8
  9.4 0.0 copy-start.9
  9.4 0.7 copy-done.9
  10.1 62.9 %shard_map.109.columns = f32[2,128,256]{2,1,0:T(8,128)S(1)} custom-call(f32[2,16,32,256]{3,2,1,0:T(8,128)S(1)} %copy-done.1, f32[2,256,256]{2,1,0:T(8,128)S(1)} %copy-done.5, bf16[2,3,16,32,256]{4,3,2,1,0:T(8,128)(2,1)} %proj_h.1, f32[2,3,3]{2,1,0:T(4,128)S(1)} %copy.12.coup, f32[3,64]{1,0:T(4,128)S(1)} %copy-done.8, s32[1,64]{1,0:T(1,128)S(1)} %bitcast.1, ...), custom_call_target="tpu_custom_call" | custom-call | tf_op jit(solution)/shard_map/pallas_call | solution.py:425
  73.0 0.0 copy-start
  73.0 0.7 copy-done
  73.7 2.0 %shard_map.110 = f32[2,16,32,256]{3,2,1,0:T(8,128)} custom-call(f32[2,128,256]{2,1,0:T(8,128)} %copy-done), custom_call_target="tpu_custom_call" | custom-call | tf_op jit(solution)/shard_map/pallas_call | solution.py:466
Async XLA Ops:
  0.7 1.2 %copy-start.1 = (f32[2,16,32,256]{3,2,1,0:T(8,128)S(1)}, f32[2,16,32,256]{3,2,1,0:T(8,128)}, u32[]{:S(2)}) copy-start(f32[2,16,32,256]{3,2,1,0:T(8,128)} %psi_h.1) | copy-start | bytes 3145732
  1.9 1.2 %copy-start.2 = (bf16[2,1024,256]{2,1,0:T(8,128)(2,1)S(1)}, bf16[2,1024,256]{2,1,0:T(8,128)(2,1)}, u32[]{:S(2)}) copy-start(bf16[2,1024,256]{2,1,0:T(8,128)(2,1)} %constant.12.clone.t1t_h) | copy-start | bytes 3145732
  3.1 1.2 %copy-start.3 = (bf16[2,256,1024]{2,1,0:T(8,128)(2,1)S(1)}, bf16[2,256,1024]{2,1,0:T(8,128)(2,1)}, u32[]{:S(2)}) copy-start(bf16[2,256,1024]{2,1,0:T(8,128)(2,1)} %constant.11.clone.t1_h) | copy-start | bytes 3145732
  4.4 1.2 %copy-start.4 = (bf16[2,512,512]{2,1,0:T(8,128)(2,1)S(1)}, bf16[2,512,512]{2,1,0:T(8,128)(2,1)}, u32[]{:S(2)}) copy-start(bf16[2,512,512]{2,1,0:T(8,128)(2,1)} %constant.10.clone.tz_h) | copy-start | bytes 3145732
  5.6 1.0 %copy-start.5 = (f32[2,256,256]{2,1,0:T(8,128)S(1)}, f32[2,256,256]{2,1,0:T(8,128)}, u32[]{:S(2)}) copy-start(f32[2,256,256]{2,1,0:T(8,128)} %pot_h.1) | copy-start | bytes 1572868
  6.6 1.0 %copy-start.6 = (f32[2,128,512]{2,1,0:T(8,128)S(1)}, f32[2,128,512]{2,1,0:T(8,128)}, u32[]{:S(2)}) copy-start(f32[2,128,512]{2,1,0:T(8,128)} %constant.14.clone.t2_h) | copy-start | bytes 1572868
  7.7 1.0 %copy-start.7 = (bf16[4,256,256]{2,1,0:T(8,128)(2,1)S(1)}, bf16[4,256,256]{2,1,0:T(8,128)(2,1)}, u32[]{:S(2)}) copy-start(bf16[4,256,256]{2,1,0:T(8,128)(2,1)} %constant.13.clone.e_h) | copy-start | bytes 1572868
  8.7 0.7 copy-start.8
  9.4 0.7 copy-start.9
  73.0 0.7 copy-start

commit v2 on v1

--- a/solution.py
+++ b/solution.py
@@ -137,12 +137,12 @@
 
 
 def kernel(
-    psi_h, pot_h, proj_h, coup, pos, spec, tz_h, t1_h, t1t_h, e_h, t2_h,
+    psi_h, pot_h, proj_h, coup_h, pos_h, spec_h, tz_h, t1_h, t1t_h, e_h, t2_h,
     out,
-    psi, pot, proj, tz, t1, t1t, e, t2,
+    psi, pot, proj, coup, pos, spec, tz, t1, t1t, e, t2,
     xs, pf, pz, pxy, vt, nl,
     zs, r1, s2, r2, s3, r3, s4, r4, ar0, ar1, ar2,
-    load_sem, sx, rx, sy, ry,
+    load_sem, sems,
 ):
     gx = lax.axis_index("gx")
     gy = lax.axis_index("gy")
@@ -159,6 +159,9 @@
         (t2_h, t2),
         (e_h, e),
         (t1t_h, t1t),
+        (pos_h, pos),
+        (spec_h, spec),
+        (coup_h, coup),
     ]
     for i, (src, dst) in enumerate(pairs):
         loads.append(pltpu.make_async_copy(src, dst, load_sem.at[i]))
@@ -178,37 +181,38 @@
             barrier, inc=1, device_id={"gy": lax.rem(gy + d, GY)}, device_id_type=MESH
         )
 
-    def over_x(slot, d, source, target):
-        peer = lax.rem(gx + d, GX)
-        return pltpu.make_async_remote_copy(
-            src_ref=source(peer),
-            dst_ref=target(gx),
-            send_sem=sx.at[slot, d],
-            recv_sem=rx.at[slot, d],
-            device_id={"gx": peer},
-            device_id_type=MESH,
-        )
-
-    def over_y(slot, d, source, target):
-        peer = lax.rem(gy + d, GY)
-        return pltpu.make_async_remote_copy(
-            src_ref=source(peer),
-            dst_ref=target(gy),
-            send_sem=sy.at[slot, d],
-            recv_sem=ry.at[slot, d],
-            device_id={"gy": peer},
-            device_id_type=MESH,
-        )
-
-    def send(over, count, slot, source, target):
-        @pl.loop(1, count)
-        def _(d):
-            over(slot, d, source, target).start()
-
-    def receive(over, count, slot, source, target):
-        @pl.loop(1, count)
-        def _(d):
-            over(slot, d, source, target).wait()
+    def exchange(axis, me, count, slot, source, target, block, landing):
+        send_sem, recv_sem = sems.at[2 * slot], sems.at[2 * slot + 1]
+
+        def post(d):
+            peer = lax.rem(me + d, count)
+            pltpu.make_async_remote_copy(
+                src_ref=source(peer),
+                dst_ref=target(me),
+                send_sem=send_sem,
+                recv_sem=recv_sem,
+                device_id={axis: peer},
+                device_id_type=MESH,
+            ).start()
+
+        for k in range(1, count):
+            d = count // 2 - k // 2 if k % 2 == 1 else count // 2 + k // 2
+            post(d)
+        pltpu.make_async_copy(source(me), target(me), recv_sem).start()
+
+        def sent():
+            pltpu.make_async_copy(block, block, send_sem).wait()
+
+        def landed():
+            pltpu.make_async_copy(landing, landing, recv_sem).wait()
+
+        return sent, landed
+
+    def over_x(*args):
+        return exchange("gx", gx, GX, *args)
+
+    def over_y(*args):
+        return exchange("gy", gy, GY, *args)
 
     def rows16(i):
         return pl.ds(pl.multiple_of(i * 16, 16), 16)
@@ -233,19 +237,25 @@
         rows = pl.ds(256 * t, 256)
         return tz[0, rows, :], tz[1, rows, :]
 
-    p1 = [(lambda p, t=t: zs.at[t, p], lambda m, t=t: r1.at[t, rows16(m)]) for t in range(2)]
-    p2 = [(lambda p, t=t: s2.at[t, p], lambda m, t=t: r2.at[t, m]) for t in range(2)]
-    p3 = [(lambda p, t=t: s3.at[t, p], lambda m, t=t: r3.at[t, rows32(m)]) for t in range(2)]
-    p4 = [(lambda p, t=t: s4.at[t, p], lambda m, t=t: r4.at[t, m]) for t in range(2)]
-
-    for t in range(2):
-        lines = product(tz_parts(t), x_parts, ((1,), (1,)))
-        zs[t] = lines.reshape(GX, 16, COLS)
-        if t == 0:
-            pl.semaphore_wait(barrier, GX + GY - 2)
-        send(over_x, GX, t, *p1[t])
-        r1[t, rows16(gx), :] = zs[t, gx]
-
+    few_x, few_y = pl.ds(0, GX - 1), pl.ds(0, GY - 1)
+
+    def post1(t):
+        return over_x(
+            t, lambda p: zs.at[t, p], lambda m: r1.at[t, rows16(m)],
+            zs.at[t, few_x], r1.at[t],
+        )
+
+    def lines(t):
+        zs[t] = product(tz_parts(t), x_parts, ((1,), (1,))).reshape(GX, 16, COLS)
+
+    lines(0)
+    pl.semaphore_wait(barrier, GX + GY - 2)
+    sent1, landed1 = [None, None], [None, None]
+    sent1[0], landed1[0] = post1(0)
+    lines(1)
+    loads[11].wait()
+    loads[12].wait()
+    loads[13].wait()
     atoms2 = jnp.concatenate([pos[...], pos[...]], axis=1)
     half = iota((1, 2 * ATOMS), 1) >= ATOMS
     quarter = jnp.where(half, 0.25, 0.0)
@@ -283,10 +293,9 @@
         chosen = jnp.where(species == 0, sums[q], sums[LPROJ + q]) * norm
         part = jnp.where(sub == q, chosen, part)
     ar0[0] = part
-    ar1[gx] = part
-    a1 = (lambda p: ar0.at[0], lambda m: ar1.at[m])
-    a2 = (lambda p: ar0.at[1], lambda m: ar2.at[m])
-    send(over_x, GX, 4, *a1)
+    sent_a1, landed_a1 = over_x(
+        8, lambda p: ar0.at[0], lambda m: ar1.at[m], ar1.at[few_x], ar1
+    )
 
     loads[5].wait()
     loads[6].wait()
@@ -306,16 +315,21 @@
                     y1 = 4 * hy + r
                     vt[t, pl.ds(16 * y1, 16), pl.ds(128 * block, 128)] = tile
 
+    sent1[0]()
+    sent1[0] = lambda: None
+    sent1[1], landed1[1] = post1(1)
+
     def pass_on(t):
-        receive(over_x, GX, t, *p1[t])
+        landed1[t]()
         for g in range(GY):
             for c in range(2):
                 s2[t, g, pl.ds(16 * c, 16), :] = r1[t, pl.ds(8 * c + g, 16, stride=16), :]
-        send(over_y, GY, t, *p2[t])
-        r2[t, gy] = s2[t, gy]
+        return over_y(
+            2 + t, lambda p: s2.at[t, p], lambda m: r2.at[t, m], s2.at[t, few_y], r2.at[t]
+        )
 
     def plane(t):
-        receive(over_y, GY, t, *p2[t])
+        landed2[t]()
         values = jnp.concatenate(
             [r2[t, :, 0:16, :].reshape(COLS, COLS), r2[t, :, 16:32, :].reshape(COLS, COLS)],
             axis=1,
@@ -336,43 +350,50 @@
         back = product(split(turned), (t1t[0], t1t[1]))
         s3[t, :, 0:16, :] = back[:, :128].reshape(GY, 16, COLS)
         s3[t, :, 16:32, :] = back[:, 128:].reshape(GY, 16, COLS)
-        send(over_y, GY, 2 + t, *p3[t])
-        r3[t, rows32(gy), :] = s3[t, gy]
+        return over_y(
+            4 + t, lambda p: s3.at[t, p], lambda m: r3.at[t, rows32(m)],
+            s3.at[t, few_y], r3.at[t],
+        )
 
     def return_on(t):
-        receive(over_y, GY, 2 + t, *p3[t])
+        landed3[t]()
         for g in range(GX):
             for c in range(2):
                 s4[t, g, pl.ds(8 * c, 8), :] = r3[t, pl.ds(16 * c + g, 8, stride=32), :]
-        send(over_x, GX, 2 + t, *p4[t])
-        r4[t, gx] = s4[t, gx]
-
-    pass_on(0)
-    receive(over_x, GX, 4, *a1)
+        return over_x(
+            6 + t, lambda p: s4.at[t, p], lambda m: r4.at[t, m], s4.at[t, few_x], r4.at[t]
+        )
+
+    sent2, landed2 = [None, None], [None, None]
+    sent3, landed3 = [None, None], [None, None]
+    sent4, landed4 = [None, None], [None, None]
+    sent2[0], landed2[0] = pass_on(0)
+    landed_a1()
     total = ar1[0]
     for g in range(1, GX):
         total += ar1[g]
     ar0[1] = total
-    ar2[gy] = total
-    send(over_y, GY, 4, *a2)
+    sent_a2, landed_a2 = over_y(
+        9, lambda p: ar0.at[1], lambda m: ar2.at[m], ar2.at[few_y], ar2
+    )
     for i in range(7, 11):
         loads[i].wait()
-    plane(0)
-    pass_on(1)
-    return_on(0)
-    plane(1)
-    return_on(1)
-
-    receive(over_y, GY, 4, *a2)
+    sent3[0], landed3[0] = plane(0)
+    sent2[1], landed2[1] = pass_on(1)
+    sent4[0], landed4[0] = return_on(0)
+    sent3[1], landed3[1] = plane(1)
+    sent4[1], landed4[1] = return_on(1)
+
+    landed_a2()
     total = ar2[0]
     for g in range(1, GY):
         total += ar2[g]
     spread = []
     for s in range(NSPEC):
         for q in range(LPROJ):
-            weight = coup[s, q, 0] * total[0:1]
+            weight = coup[q, s : s + 1, 0:1] * total[0:1]
             for m in range(1, LPROJ):
-                weight += coup[s, q, m] * total[m : m + 1]
+                weight += coup[q, s : s + 1, m : m + 1] * total[m : m + 1]
             weight = weight * (1.0 / math.sqrt(ATOMS * LPROJ))
             spread.append(jnp.where(species == s, weight, 0.0))
     nonloc = None
@@ -387,12 +408,14 @@
 
     recip = None
     for t in range(2):
-        receive(over_x, GX, 2 + t, *p4[t])
+        landed4[t]()
         lines = r4[t].reshape(256, COLS)
         term = product(split(jnp.transpose(lines)), tz_parts(t))
         recip = term if recip is None else recip + term
     for c in range(2):
         out[c] = jnp.where(inside, nl[c] + recip[:, c * N : (c + 1) * N], 0.0)
+    for sent in (*sent1, *sent2, *sent3, *sent4, sent_a1, sent_a2):
+        sent()
 
 
 def place(columns, out):
@@ -419,18 +442,20 @@
 def per_device(psi_coeff, potential, projectors, coupling, positions, species):
     f32, bf16 = jnp.float32, jnp.bfloat16
     consts = [jnp.asarray(table) for table in tables()]
-    hbm = pl.BlockSpec(memory_space=pl.ANY)
+    hbm = pl.BlockSpec(memory_space=pltpu.HBM)
     vmem = pl.BlockSpec(memory_space=pltpu.VMEM)
-    smem = pl.BlockSpec(memory_space=pltpu.SMEM)
     columns = pl.pallas_call(
         kernel,
         out_shape=jax.ShapeDtypeStruct((2, COLS, N), f32),
-        in_specs=[hbm, hbm, hbm, smem, vmem, vmem] + [hbm] * 5,
+        in_specs=[hbm] * 11,
         out_specs=vmem,
         scratch_shapes=[
             pltpu.VMEM((2, 9, 32, N), f32),
             pltpu.VMEM((2, 2, N, 128), f32),
             pltpu.VMEM((NSPEC, LPROJ, 9, 32, N), bf16),
+            pltpu.VMEM((LPROJ, NSPEC, LPROJ), f32),
+            pltpu.VMEM((3, ATOMS), f32),
+            pltpu.VMEM((1, ATOMS), jnp.int32),
             pltpu.VMEM((2, 512, 512), bf16),
             pltpu.VMEM((2, 256, 1024), bf16),
             pltpu.VMEM((2, 1024, 256), bf16),
@@ -453,16 +478,21 @@
             pltpu.VMEM((2, 8, 128), f32),
             pltpu.VMEM((GX, 8, 128), f32),
             pltpu.VMEM((GY, 8, 128), f32),
-            pltpu.SemaphoreType.DMA((11,)),
-            pltpu.SemaphoreType.DMA((5, GX)),
-            pltpu.SemaphoreType.DMA((5, GX)),
-            pltpu.SemaphoreType.DMA((5, GY)),
-            pltpu.SemaphoreType.DMA((5, GY)),
+            pltpu.SemaphoreType.DMA((14,)),
+            pltpu.SemaphoreType.DMA((20,)),
         ],
         compiler_params=pltpu.CompilerParams(
-            collective_id=0, has_side_effects=True, vmem_limit_bytes=48 * 1024 * 1024
+            collective_id=0, has_side_effects=True, vmem_limit_bytes=60 * 1024 * 1024
         ),
-    )(psi_coeff, potential, projectors, coupling, positions, species.reshape(1, ATOMS), *consts)
+    )(
+        psi_coeff,
+        potential,
+        projectors,
+        jnp.transpose(coupling, (1, 0, 2)),
+        positions,
+        species.reshape(1, ATOMS),
+        *consts,
+    )
     return pl.pallas_call(
         place,
         out_shape=jax.ShapeDtypeStruct((2, 16, 32, N), f32),

time: 76.2 us -> 55.7 us (0.73)
  local copies, waits for them, and re-layouts: 10.7 us -> 0 us
  Pallas kernels: 64.9 us -> 55.5 us
    unnamed x21 -> x0, local copies, waits for them, and re-layouts: 10.7 us -> none
    pallas_call x1, Pallas kernels: 62.9 us -> 53.5 us  [per_device(): pl.pallas_call(kernel, out_shape=jax.ShapeDtypeStruct((2, COLS, N), f32),...]
where the time goes in v2:
time: 55.7 us; the launch traced here: 55.5 us
  Pallas kernels  55.5 us (100%)
    pallas_call x1, Pallas kernels, per_device(): pl.pallas_call(kernel, out_shape=jax.ShapeDtypeStruct((2, COLS, N), f32),...  53.5 us
    pallas_call x1, Pallas kernels, per_device(): pl.pallas_call(place, out_shape=jax.ShapeDtypeStruct((2, 16, 32, N), f32)...  1.99 us

profile of v2, /device:TPU:1, one launch (start us, length us, event | category | flops | bytes accessed | tf_op | source)
XLA Modules:
  0.0 55.5 jit_solution(10830384391305607993)
XLA Ops:
  0.0 53.5 %shard_map.109.columns = f32[2,128,256]{2,1,0:T(8,128)} custom-call(f32[2,16,32,256]{3,2,1,0:T(8,128)} %psi_h.1, f32[2,256,256]{2,1,0:T(8,128)} %pot_h.1, bf16[2,3,16,32,256]{4,3,2,1,0:T(8,128)(2,1)} %proj_h.1, f32[3,2,3]{2,1,0:T(2,128)} %bitcast.2, f32[3,64]{1,0:T(4,128)} %pos_h.1, s32[1,64]{1,0:T(1,128)} %bitcast.3, ...), custom_call_target="tpu_custom_call" | custom-call | tf_op jit(solution)/shard_map/pallas_call | solution.py:447
  53.5 2.0 %shard_map.110 = f32[2,16,32,256]{3,2,1,0:T(8,128)} custom-call(f32[2,128,256]{2,1,0:T(8,128)} %shard_map.109.columns), custom_call_target="tpu_custom_call" | custom-call | tf_op jit(solution)/shard_map/pallas_call | solution.py:496

commit v3 on v2

--- a/solution.py
+++ b/solution.py
@@ -45,8 +45,8 @@
 
 @functools.lru_cache(maxsize=None)
 def tables():
-    t, g, c, y = np.meshgrid(
-        np.arange(2), np.arange(GX), np.arange(2), np.arange(GY), indexing="ij"
+    t, g, y, c = np.meshgrid(
+        np.arange(2), np.arange(GX), np.arange(GY), np.arange(2), indexing="ij"
     )
     z = (16 * g + 2 * y + t).reshape(-1, 1)
     c = c.reshape(-1, 1)
@@ -141,8 +141,8 @@
     out,
     psi, pot, proj, coup, pos, spec, tz, t1, t1t, e, t2,
     xs, pf, pz, pxy, vt, nl,
-    zs, r1, s2, r2, s3, r3, s4, r4, ar0, ar1, ar2,
-    load_sem, sems,
+    zs, r2, s3, r4, ar0, ar1, ar2,
+    load_sem, sems, ready,
 ):
     gx = lax.axis_index("gx")
     gy = lax.axis_index("gy")
@@ -165,21 +165,19 @@
     ]
     for i, (src, dst) in enumerate(pairs):
         loads.append(pltpu.make_async_copy(src, dst, load_sem.at[i]))
-        loads[-1].start()
-
+    for load in loads[:3]:
+        load.start()
     barrier = pltpu.get_barrier_semaphore()
-
-    @pl.loop(1, GX)
-    def _(d):
+    for d in range(1, GX):
         pl.semaphore_signal(
             barrier, inc=1, device_id={"gx": lax.rem(gx + d, GX)}, device_id_type=MESH
         )
-
-    @pl.loop(1, GY)
-    def _(d):
+    for d in range(1, GY):
         pl.semaphore_signal(
             barrier, inc=1, device_id={"gy": lax.rem(gy + d, GY)}, device_id_type=MESH
         )
+    for load in loads[3:]:
+        load.start()
 
     def exchange(axis, me, count, slot, source, target, block, landing):
         send_sem, recv_sem = sems.at[2 * slot], sems.at[2 * slot + 1]
@@ -214,11 +212,53 @@
     def over_y(*args):
         return exchange("gy", gy, GY, *args)
 
-    def rows16(i):
-        return pl.ds(pl.multiple_of(i * 16, 16), 16)
-
-    def rows32(i):
-        return pl.ds(pl.multiple_of(i * 32, 32), 32)
+    by_x = [lax.rem(gx + d, GX) for d in range(GX)]
+    by_y = [lax.rem(gy + d, GY) for d in range(GY)]
+
+    def exchange_all(slot, source, target, source_at, target_at):
+        send_sem, recv_sem = sems.at[2 * slot], sems.at[2 * slot + 1]
+        mine = target.at[pl.ds(target_at(gx, gy), 2), :]
+
+        def post(px, py):
+            pltpu.make_async_remote_copy(
+                src_ref=source.at[pl.ds(source_at(px, py), 2), :],
+                dst_ref=mine,
+                send_sem=send_sem,
+                recv_sem=recv_sem,
+                device_id={"gx": px, "gy": py},
+                device_id_type=MESH,
+            ).start()
+
+        for py in by_y:
+            post(by_x[8], py)
+
+        @pl.loop(1, 8)
+        def _(j):
+            one, other = lax.rem(gx + (8 - j), GX), lax.rem(gx + (8 + j), GX)
+            for py in by_y:
+                post(one, py)
+                post(other, py)
+
+        for py in by_y[1:]:
+            post(gx, py)
+        pltpu.make_async_copy(
+            source.at[pl.ds(source_at(gx, gy), 2), :], mine, recv_sem
+        ).start()
+
+        def sent():
+            block = source.at[pl.ds(0, 254), :]
+            pltpu.make_async_copy(block, block, send_sem).wait()
+
+        def landed():
+            pltpu.make_async_copy(target, target, recv_sem).wait()
+
+        return sent, landed
+
+    def by_gx(px, py):
+        return (px * GY + py) * 2
+
+    def by_gy(px, py):
+        return (py * GX + px) * 2
 
     kx, ky = column_freqs(gx, gy, (COLS, N))
     lane = iota((COLS, N), 1)
@@ -239,20 +279,21 @@
 
     few_x, few_y = pl.ds(0, GX - 1), pl.ds(0, GY - 1)
 
-    def post1(t):
-        return over_x(
-            t, lambda p: zs.at[t, p], lambda m: r1.at[t, rows16(m)],
-            zs.at[t, few_x], r1.at[t],
-        )
-
     def lines(t):
-        zs[t] = product(tz_parts(t), x_parts, ((1,), (1,))).reshape(GX, 16, COLS)
+        zs[t] = product(tz_parts(t), x_parts, ((1,), (1,)))
+
+    def scatter(t):
+        return exchange_all(t, zs.at[t], r2.at[t], by_gx, by_gy)
 
     lines(0)
     pl.semaphore_wait(barrier, GX + GY - 2)
+    for py in by_y[1:]:
+        pl.semaphore_signal(ready, inc=1, device_id={"gy": py}, device_id_type=MESH)
+    lines(1)
+    pl.semaphore_wait(ready, GY - 1)
     sent1, landed1 = [None, None], [None, None]
-    sent1[0], landed1[0] = post1(0)
-    lines(1)
+    sent1[0], landed1[0] = scatter(0)
+
     loads[11].wait()
     loads[12].wait()
     loads[13].wait()
@@ -294,7 +335,7 @@
         part = jnp.where(sub == q, chosen, part)
     ar0[0] = part
     sent_a1, landed_a1 = over_x(
-        8, lambda p: ar0.at[0], lambda m: ar1.at[m], ar1.at[few_x], ar1
+        4, lambda p: ar0.at[0], lambda m: ar1.at[m], ar1.at[few_x], ar1
     )
 
     loads[5].wait()
@@ -316,23 +357,12 @@
                     vt[t, pl.ds(16 * y1, 16), pl.ds(128 * block, 128)] = tile
 
     sent1[0]()
-    sent1[0] = lambda: None
-    sent1[1], landed1[1] = post1(1)
-
-    def pass_on(t):
+    sent1[1], landed1[1] = scatter(1)
+
+    def plane(t):
         landed1[t]()
-        for g in range(GY):
-            for c in range(2):
-                s2[t, g, pl.ds(16 * c, 16), :] = r1[t, pl.ds(8 * c + g, 16, stride=16), :]
-        return over_y(
-            2 + t, lambda p: s2.at[t, p], lambda m: r2.at[t, m], s2.at[t, few_y], r2.at[t]
-        )
-
-    def plane(t):
-        landed2[t]()
         values = jnp.concatenate(
-            [r2[t, :, 0:16, :].reshape(COLS, COLS), r2[t, :, 16:32, :].reshape(COLS, COLS)],
-            axis=1,
+            [r2[t, pl.ds(0, COLS, stride=2), :], r2[t, pl.ds(1, COLS, stride=2), :]], axis=1
         )
         lanes = product(split(values), (t1[0], t1[1]))
         lanes_re, lanes_im = lanes[:, :512], lanes[:, 512:]
@@ -348,41 +378,27 @@
             [rows_re * cos + rows_im * sin, rows_im * cos - rows_re * sin], axis=1
         )
         back = product(split(turned), (t1t[0], t1t[1]))
-        s3[t, :, 0:16, :] = back[:, :128].reshape(GY, 16, COLS)
-        s3[t, :, 16:32, :] = back[:, 128:].reshape(GY, 16, COLS)
-        return over_y(
-            4 + t, lambda p: s3.at[t, p], lambda m: r3.at[t, rows32(m)],
-            s3.at[t, few_y], r3.at[t],
-        )
-
-    def return_on(t):
-        landed3[t]()
-        for g in range(GX):
-            for c in range(2):
-                s4[t, g, pl.ds(8 * c, 8), :] = r3[t, pl.ds(16 * c + g, 8, stride=32), :]
-        return over_x(
-            6 + t, lambda p: s4.at[t, p], lambda m: r4.at[t, m], s4.at[t, few_x], r4.at[t]
-        )
-
-    sent2, landed2 = [None, None], [None, None]
-    sent3, landed3 = [None, None], [None, None]
+        s3[t, pl.ds(0, COLS, stride=2), :] = back[:, :128]
+        s3[t, pl.ds(1, COLS, stride=2), :] = back[:, 128:]
+
+    def gather(t):
+        return exchange_all(2 + t, s3.at[t], r4.at[t], by_gy, by_gx)
+
     sent4, landed4 = [None, None], [None, None]
-    sent2[0], landed2[0] = pass_on(0)
     landed_a1()
     total = ar1[0]
     for g in range(1, GX):
         total += ar1[g]
     ar0[1] = total
     sent_a2, landed_a2 = over_y(
-        9, lambda p: ar0.at[1], lambda m: ar2.at[m], ar2.at[few_y], ar2
+        5, lambda p: ar0.at[1], lambda m: ar2.at[m], ar2.at[few_y], ar2
     )
     for i in range(7, 11):
         loads[i].wait()
-    sent3[0], landed3[0] = plane(0)
-    sent2[1], landed2[1] = pass_on(1)
-    sent4[0], landed4[0] = return_on(0)
-    sent3[1], landed3[1] = plane(1)
-    sent4[1], landed4[1] = return_on(1)
+    plane(0)
+    sent4[0], landed4[0] = gather(0)
+    plane(1)
+    sent4[1], landed4[1] = gather(1)
 
     landed_a2()
     total = ar2[0]
@@ -409,34 +425,47 @@
     recip = None
     for t in range(2):
         landed4[t]()
-        lines = r4[t].reshape(256, COLS)
-        term = product(split(jnp.transpose(lines)), tz_parts(t))
+        term = product(split(jnp.transpose(r4[t])), tz_parts(t))
         recip = term if recip is None else recip + term
     for c in range(2):
-        out[c] = jnp.where(inside, nl[c] + recip[:, c * N : (c + 1) * N], 0.0)
-    for sent in (*sent1, *sent2, *sent3, *sent4, sent_a1, sent_a2):
+        value = jnp.where(inside, nl[c] + recip[:, c * N : (c + 1) * N], 0.0)
+        col = iota((COLS, N), 0)
+        corner = (col == COL_X) | (col == COL_Y)
+        regular = jnp.where(corner, 0.0, value).reshape(8, 2, 8, N)
+        sub = iota((8, N), 0)
+        for half in range(2):
+            out[c, pl.ds(8 * half, 8)] = regular[:, half]
+        for place, special in ((16, COL_X), (17, COL_Y)):
+            row = jnp.broadcast_to(value[special : special + 1], (8, N))
+            out[c, place] = jnp.where(sub == 0, row, 0.0)
+    for sent in (sent1[1], *sent4, sent_a1, sent_a2):
         sent()
 
 
-def place(columns, out):
-    sub = iota((8, N), 0)
+def place(tiles, out, held, zeros, load_sem, sem):
+    load = pltpu.make_async_copy(tiles, held, load_sem)
+    load.start()
+    copies = []
+
+    def put(src, dst):
+        copies.append(pltpu.make_async_copy(src, dst, sem.at[len(copies)]))
+        copies[-1].start()
+
+    zeros[...] = jnp.zeros_like(zeros)
     for c in range(2):
-        for row in range(16):
-            if row in ROWS_X:
-                base = 16 * ROWS_X.index(row)
-                out[c, row, 0:8, :] = columns[c, base : base + 8, :]
-                out[c, row, 8:24, :] = jnp.zeros((16, N), jnp.float32)
-                out[c, row, 24:32, :] = columns[c, base + 8 : base + 16, :]
-            else:
-                out[c, row] = jnp.zeros((32, N), jnp.float32)
-        along_y = jnp.broadcast_to(columns[c, COL_Y : COL_Y + 1, :], (8, N))
-        out[c, 0, 8:16, :] = jnp.where(sub == 0, along_y, 0.0)
-        along_x = jnp.broadcast_to(columns[c, COL_X : COL_X + 1, :], (8, N))
-        out[c, 4, 0:8, :] = jnp.where(sub == 0, along_x, 0.0)
-        corner = columns[c, 64:72, :]
-        out[c, 12, 0:8, :] = jnp.where(sub == 7, 0.0, corner)
-        corner = columns[c, 72:80, :]
-        out[c, 12, 24:32, :] = jnp.where(sub == 0, 0.0, corner)
+        put(zeros, out.at[c, 5:12])
+        put(zeros.at[0, 8:32], out.at[c, 4, 8:32])
+        put(zeros.at[0:3, 8:24], out.at[c, 1:4, 8:24])
+        put(zeros.at[0:4, 8:24], out.at[c, 12:16, 8:24])
+        put(zeros.at[0, 16:24], out.at[c, 0, 16:24])
+    load.wait()
+    for half, rows in enumerate((pl.ds(0, 8), pl.ds(24, 8))):
+        put(held.at[:, pl.ds(8 * half, 4)], out.at[:, 0:4, rows])
+        put(held.at[:, pl.ds(8 * half + 4, 4)], out.at[:, 12:16, rows])
+    put(held.at[:, 16], out.at[:, 4, 0:8])
+    put(held.at[:, 17], out.at[:, 0, 8:16])
+    for copy in copies:
+        copy.wait()
 
 
 def per_device(psi_coeff, potential, projectors, coupling, positions, species):
@@ -446,7 +475,7 @@
     vmem = pl.BlockSpec(memory_space=pltpu.VMEM)
     columns = pl.pallas_call(
         kernel,
-        out_shape=jax.ShapeDtypeStruct((2, COLS, N), f32),
+        out_shape=jax.ShapeDtypeStruct((2, 18, 8, N), f32),
         in_specs=[hbm] * 11,
         out_specs=vmem,
         scratch_shapes=[
@@ -467,19 +496,16 @@
             pltpu.VMEM((2, COLS, 2 * ATOMS), f32),
             pltpu.VMEM((2, 128, 512), f32),
             pltpu.VMEM((2, COLS, N), f32),
-            pltpu.VMEM((2, GX, 16, COLS), f32),
-            pltpu.VMEM((2, GX * 16, COLS), f32),
-            pltpu.VMEM((2, GY, 32, COLS), f32),
-            pltpu.VMEM((2, GY, 32, COLS), f32),
-            pltpu.VMEM((2, GY, 32, COLS), f32),
-            pltpu.VMEM((2, GY * 32, COLS), f32),
-            pltpu.VMEM((2, GX, 16, COLS), f32),
-            pltpu.VMEM((2, GX, 16, COLS), f32),
+            pltpu.VMEM((2, 256, COLS), f32),
+            pltpu.VMEM((2, 256, COLS), f32),
+            pltpu.VMEM((2, 256, COLS), f32),
+            pltpu.VMEM((2, 256, COLS), f32),
             pltpu.VMEM((2, 8, 128), f32),
             pltpu.VMEM((GX, 8, 128), f32),
             pltpu.VMEM((GY, 8, 128), f32),
             pltpu.SemaphoreType.DMA((14,)),
-            pltpu.SemaphoreType.DMA((20,)),
+            pltpu.SemaphoreType.DMA((12,)),
+            pltpu.SemaphoreType.REGULAR,
         ],
         compiler_params=pltpu.CompilerParams(
             collective_id=0, has_side_effects=True, vmem_limit_bytes=60 * 1024 * 1024
@@ -496,8 +522,15 @@
     return pl.pallas_call(
         place,
         out_shape=jax.ShapeDtypeStruct((2, 16, 32, N), f32),
-        in_specs=[vmem],
-        out_specs=vmem,
+        in_specs=[hbm],
+        out_specs=hbm,
+        scratch_shapes=[
+            pltpu.VMEM((2, 18, 8, N), f32),
+            pltpu.VMEM((7, 32, N), f32),
+            pltpu.SemaphoreType.DMA,
+            pltpu.SemaphoreType.DMA((16,)),
+        ],
+        compiler_params=pltpu.CompilerParams(vmem_limit_bytes=60 * 1024 * 1024),
     )(columns)
 
 

time: 55.7 us -> 52.5 us (0.943)
  Pallas kernels: 55.5 us -> 52.3 us
    pallas_call x1, Pallas kernels: 53.5 us -> 50.4 us  [per_device(): pl.pallas_call(kernel, out_shape=jax.ShapeDtypeStruct((2, 18, 8, N), f32)...]
where the time goes in v3:
time: 52.5 us; the launch traced here: 52.4 us
  Pallas kernels  52.3 us (100%)
    pallas_call x1, Pallas kernels, per_device(): pl.pallas_call(kernel, out_shape=jax.ShapeDtypeStruct((2, 18, 8, N), f32)...  50.4 us
    pallas_call x1, Pallas kernels, per_device(): pl.pallas_call(place, out_shape=jax.ShapeDtypeStruct((2, 16, 32, N), f32)...  1.96 us

profile of v3, /device:TPU:1, one launch (start us, length us, event | category | flops | bytes accessed | tf_op | source)
XLA Modules:
  0.0 52.4 jit_solution(8035255012561386627)
XLA Ops:
  0.0 50.4 %shard_map.109.tiles = f32[2,18,8,256]{3,2,1,0:T(8,128)} custom-call(f32[2,16,32,256]{3,2,1,0:T(8,128)} %psi_h.1, f32[2,256,256]{2,1,0:T(8,128)} %pot_h.1, bf16[2,3,16,32,256]{4,3,2,1,0:T(8,128)(2,1)} %proj_h.1, f32[3,2,3]{2,1,0:T(2,128)} %bitcast.2, f32[3,64]{1,0:T(4,128)} %pos_h.1, s32[1,64]{1,0:T(1,128)} %bitcast.3, ...), custom_call_target="tpu_custom_call" | custom-call | tf_op jit(solution)/shard_map/pallas_call | solution.py:476
  50.4 2.0 %shard_map.110 = f32[2,16,32,256]{3,2,1,0:T(8,128)} custom-call(f32[2,18,8,256]{3,2,1,0:T(8,128)} %shard_map.109.tiles), custom_call_target="tpu_custom_call" | custom-call | tf_op jit(solution)/shard_map/pallas_call | solution.py:522

commit v4 on v3

--- a/solution.py
+++ b/solution.py
@@ -24,6 +24,7 @@
 HELD_X = (0, 1, 2, 3, 5, 6, 7, 8)
 COL_Y = 71
 COL_X = 72
+COL_Z = 73
 
 
 def column_offsets(col):
@@ -119,6 +120,13 @@
 
 def fractional(product_):
     return product_ - jnp.floor(product_)
+
+
+def inner(value):
+    row, lane = iota((COLS, COLS), 0), iota((COLS, COLS), 1)
+    both = jnp.where(lane < RADIUS, value[:, :COLS], value[:, COLS:])
+    extra = jnp.broadcast_to(value[0:1, RADIUS : RADIUS + 1], (COLS, COLS))
+    return jnp.where((row == COL_Z) & (lane == 0), extra, both)
 
 
 def pick_columns(held):
@@ -229,21 +237,22 @@
                 device_id_type=MESH,
             ).start()
 
-        for py in by_y:
-            post(by_x[8], py)
-
-        @pl.loop(1, 8)
-        def _(j):
-            one, other = lax.rem(gx + (8 - j), GX), lax.rem(gx + (8 + j), GX)
-            for py in by_y:
-                post(one, py)
-                post(other, py)
-
-        for py in by_y[1:]:
-            post(gx, py)
-        pltpu.make_async_copy(
-            source.at[pl.ds(source_at(gx, gy), 2), :], mine, recv_sem
-        ).start()
+        def step(j):
+            @pl.loop(0, GY)
+            def _(d):
+                py = lax.rem(gy + d, GY)
+                post(by_x[8 - j], py)
+                if j > 0:
+                    post(by_x[8 + j], py)
+
+        def last():
+            for py in by_y[1:]:
+                post(gx, py)
+            pltpu.make_async_copy(
+                source.at[pl.ds(source_at(gx, gy), 2), :], mine, recv_sem
+            ).start()
+
+        steps = [functools.partial(step, j) for j in range(8)] + [last]
 
         def sent():
             block = source.at[pl.ds(0, 254), :]
@@ -252,7 +261,7 @@
         def landed():
             pltpu.make_async_copy(target, target, recv_sem).wait()
 
-        return sent, landed
+        return steps, sent, landed
 
     def by_gx(px, py):
         return (px * GY + py) * 2
@@ -291,8 +300,20 @@
         pl.semaphore_signal(ready, inc=1, device_id={"gy": py}, device_id_type=MESH)
     lines(1)
     pl.semaphore_wait(ready, GY - 1)
-    sent1, landed1 = [None, None], [None, None]
-    sent1[0], landed1[0] = scatter(0)
+    steps, sent1, landed1 = zip(scatter(0), scatter(1))
+    queue = [*steps[0], *steps[1]]
+
+    def proceed(count=1):
+        for _ in range(min(count, len(queue))):
+            queue.pop(0)()
+
+    proceed(3)
+    for c in range(2):
+        for row in range(16):
+            if row in ROWS_X:
+                out[c, row, 8:24, :] = jnp.zeros((16, N), jnp.float32)
+            else:
+                out[c, row] = jnp.zeros((32, N), jnp.float32)
 
     loads[11].wait()
     loads[12].wait()
@@ -300,31 +321,39 @@
     atoms2 = jnp.concatenate([pos[...], pos[...]], axis=1)
     half = iota((1, 2 * ATOMS), 1) >= ATOMS
     quarter = jnp.where(half, 0.25, 0.0)
-    row = iota((N, 2 * ATOMS), 0)
-    kz_rows = jnp.where(row < N // 2, row, row - N).astype(jnp.float32)
+    row = iota((COLS, 2 * ATOMS), 0)
+    kz_rows = jnp.where(row < RADIUS, row, row - 2 * RADIUS).astype(jnp.float32)
     turns_z = fractional(kz_rows * atoms2[2:3])
     pz_f32 = jnp.concatenate(
         [cos_turns(turns_z - quarter), cos_turns(turns_z + (0.25 - quarter))], axis=0
     )
     pz[0], pz[1] = split(pz_f32)
+    proceed()
     kx_col, ky_col = column_freqs(gx, gy, (COLS, 2 * ATOMS))
     turns_xy = fractional(kx_col.astype(jnp.float32) * atoms2[0:1]) + fractional(
         ky_col.astype(jnp.float32) * atoms2[1:2]
     )
+    turns_xy = jnp.where(row == COL_Z, fractional(RADIUS * atoms2[2:3]), turns_xy)
     pxy[0] = cos_turns(turns_xy)
     pxy[1] = cos_turns(turns_xy + jnp.where(half, -0.25, 0.25))
+    proceed()
 
     loads[3].wait()
     loads[4].wait()
     pz_parts = (pz[0], pz[1])
+    inner_re, inner_im = inner(xs[0]), inner(xs[1])
     sums = []
     for s in range(NSPEC):
+        weighted = []
         for q in range(LPROJ):
-            factor = pick_columns(lambda i: proj[s, q, i].astype(jnp.float32))
+            factor = inner(pick_columns(lambda i: proj[s, q, i].astype(jnp.float32)))
             pf[s * LPROJ + q] = factor
-            weighted = jnp.concatenate([factor * xs[0], factor * xs[1]], axis=1)
-            along_z = product(split(weighted), pz_parts)
-            along = along_z * pxy[0] + pltpu.roll(along_z, ATOMS, 1) * pxy[1]
+            weighted.append(jnp.concatenate([factor * inner_re, factor * inner_im], axis=1))
+            proceed(3)
+        along_z = product(split(jnp.concatenate(weighted, axis=0)), pz_parts)
+        for q in range(LPROJ):
+            part = along_z[COLS * q : COLS * (q + 1)]
+            along = part * pxy[0] + pltpu.roll(part, ATOMS, 1) * pxy[1]
             sums.append(jnp.sum(along, axis=0, keepdims=True))
     species = jnp.concatenate([spec[...], spec[...]], axis=1)
     norm = 4.0 / math.sqrt(N * N * N)
@@ -355,9 +384,7 @@
                         tile = moved if tile is None else jnp.where(lane16 >= 32 * j, moved, tile)
                     y1 = 4 * hy + r
                     vt[t, pl.ds(16 * y1, 16), pl.ds(128 * block, 128)] = tile
-
-    sent1[0]()
-    sent1[1], landed1[1] = scatter(1)
+        proceed(1)
 
     def plane(t):
         landed1[t]()
@@ -365,14 +392,17 @@
             [r2[t, pl.ds(0, COLS, stride=2), :], r2[t, pl.ds(1, COLS, stride=2), :]], axis=1
         )
         lanes = product(split(values), (t1[0], t1[1]))
+        proceed(2)
         lanes_re, lanes_im = lanes[:, :512], lanes[:, 512:]
         cos, sin = t2[0], t2[1]
         turned = jnp.concatenate(
             [lanes_re * cos - lanes_im * sin, lanes_re * sin + lanes_im * cos], axis=0
         )
         space = product((e[0], e[1]), split(turned))
+        proceed(2)
         field = jnp.concatenate([space[:128] * vt[t], space[128:] * vt[t]], axis=0)
         rows = product((e[2], e[3]), split(field))
+        proceed(2)
         rows_re, rows_im = rows[:128], rows[128:]
         turned = jnp.concatenate(
             [rows_re * cos + rows_im * sin, rows_im * cos - rows_re * sin], axis=1
@@ -384,7 +414,14 @@
     def gather(t):
         return exchange_all(2 + t, s3.at[t], r4.at[t], by_gy, by_gx)
 
-    sent4, landed4 = [None, None], [None, None]
+    steps4, sent4, landed4 = zip(gather(0), gather(1))
+    for i in range(7, 11):
+        loads[i].wait()
+    proceed(9)
+    plane(0)
+    proceed(len(queue))
+    queue += steps4[0]
+    proceed(9)
     landed_a1()
     total = ar1[0]
     for g in range(1, GX):
@@ -393,12 +430,11 @@
     sent_a2, landed_a2 = over_y(
         5, lambda p: ar0.at[1], lambda m: ar2.at[m], ar2.at[few_y], ar2
     )
-    for i in range(7, 11):
-        loads[i].wait()
-    plane(0)
-    sent4[0], landed4[0] = gather(0)
+    proceed(9)
     plane(1)
-    sent4[1], landed4[1] = gather(1)
+    proceed(len(queue))
+    queue += steps4[1]
+    proceed(9)
 
     landed_a2()
     total = ar2[0]
@@ -413,15 +449,27 @@
             weight = weight * (1.0 / math.sqrt(ATOMS * LPROJ))
             spread.append(jnp.where(species == s, weight, 0.0))
     nonloc = None
-    for i, weight in enumerate(spread):
-        around = pltpu.roll(jnp.broadcast_to(weight, (8, 2 * ATOMS)), ATOMS, 1)[0:1]
-        at_columns = pxy[0] * weight - pxy[1] * around
+    for s in range(NSPEC):
+        at_columns = []
+        for weight in spread[LPROJ * s : LPROJ * (s + 1)]:
+            around = pltpu.roll(jnp.broadcast_to(weight, (8, 2 * ATOMS)), ATOMS, 1)[0:1]
+            at_columns.append(pxy[0] * weight - pxy[1] * around)
+        at_columns = jnp.concatenate(at_columns, axis=0)
         spread_z = product(split(at_columns), pz_parts, ((1,), (1,)))
-        term = jnp.concatenate([pf[i] * spread_z[:, :N], pf[i] * spread_z[:, N:]], axis=1)
-        nonloc = term if nonloc is None else nonloc + term
+        for q in range(LPROJ):
+            factor = pf[s * LPROJ + q]
+            part = spread_z[COLS * q : COLS * (q + 1)]
+            term = jnp.concatenate([factor * part[:, :COLS], factor * part[:, COLS:]], axis=1)
+            nonloc = term if nonloc is None else nonloc + term
+        proceed(1)
+    row, lane = iota((COLS, COLS), 0), iota((COLS, COLS), 1)
     for c in range(2):
-        nl[c] = nonloc[:, c * N : (c + 1) * N] + kinetic * xs[c]
-
+        part = nonloc[:, c * COLS : (c + 1) * COLS]
+        extra = jnp.broadcast_to(part[COL_Z : COL_Z + 1, 0:1], (COLS, COLS))
+        low = jnp.where((row == 0) & (lane == RADIUS), extra, part)
+        nl[c] = jnp.concatenate([low, part], axis=1) + kinetic * xs[c]
+
+    proceed(len(queue))
     recip = None
     for t in range(2):
         landed4[t]()
@@ -429,43 +477,19 @@
         recip = term if recip is None else recip + term
     for c in range(2):
         value = jnp.where(inside, nl[c] + recip[:, c * N : (c + 1) * N], 0.0)
-        col = iota((COLS, N), 0)
-        corner = (col == COL_X) | (col == COL_Y)
-        regular = jnp.where(corner, 0.0, value).reshape(8, 2, 8, N)
+        tiles = [value[8 * k : 8 * k + 8] for k in range(16)]
         sub = iota((8, N), 0)
-        for half in range(2):
-            out[c, pl.ds(8 * half, 8)] = regular[:, half]
-        for place, special in ((16, COL_X), (17, COL_Y)):
-            row = jnp.broadcast_to(value[special : special + 1], (8, N))
-            out[c, place] = jnp.where(sub == 0, row, 0.0)
-    for sent in (sent1[1], *sent4, sent_a1, sent_a2):
+        row = jnp.broadcast_to(value[COL_X : COL_X + 1], (8, N))
+        out[c, 4, 0:8, :] = jnp.where(sub == 0, row, 0.0)
+        row = jnp.broadcast_to(value[COL_Y : COL_Y + 1], (8, N))
+        out[c, 0, 8:16, :] = jnp.where(sub == 0, row, 0.0)
+        tiles[8] = jnp.where(sub == COL_Y % 8, 0.0, tiles[8])
+        tiles[9] = jnp.where(sub == COL_X % 8, 0.0, tiles[9])
+        for k, row in enumerate(ROWS_X):
+            out[c, row, 0:8, :] = tiles[2 * k]
+            out[c, row, 24:32, :] = tiles[2 * k + 1]
+    for sent in (*sent1, *sent4, sent_a1, sent_a2):
         sent()
-
-
-def place(tiles, out, held, zeros, load_sem, sem):
-    load = pltpu.make_async_copy(tiles, held, load_sem)
-    load.start()
-    copies = []
-
-    def put(src, dst):
-        copies.append(pltpu.make_async_copy(src, dst, sem.at[len(copies)]))
-        copies[-1].start()
-
-    zeros[...] = jnp.zeros_like(zeros)
-    for c in range(2):
-        put(zeros, out.at[c, 5:12])
-        put(zeros.at[0, 8:32], out.at[c, 4, 8:32])
-        put(zeros.at[0:3, 8:24], out.at[c, 1:4, 8:24])
-        put(zeros.at[0:4, 8:24], out.at[c, 12:16, 8:24])
-        put(zeros.at[0, 16:24], out.at[c, 0, 16:24])
-    load.wait()
-    for half, rows in enumerate((pl.ds(0, 8), pl.ds(24, 8))):
-        put(held.at[:, pl.ds(8 * half, 4)], out.at[:, 0:4, rows])
-        put(held.at[:, pl.ds(8 * half + 4, 4)], out.at[:, 12:16, rows])
-    put(held.at[:, 16], out.at[:, 4, 0:8])
-    put(held.at[:, 17], out.at[:, 0, 8:16])
-    for copy in copies:
-        copy.wait()
 
 
 def per_device(psi_coeff, potential, projectors, coupling, positions, species):
@@ -473,9 +497,9 @@
     consts = [jnp.asarray(table) for table in tables()]
     hbm = pl.BlockSpec(memory_space=pltpu.HBM)
     vmem = pl.BlockSpec(memory_space=pltpu.VMEM)
-    columns = pl.pallas_call(
+    return pl.pallas_call(
         kernel,
-        out_shape=jax.ShapeDtypeStruct((2, 18, 8, N), f32),
+        out_shape=pltpu.VMEM((2, 16, 32, N), f32),
         in_specs=[hbm] * 11,
         out_specs=vmem,
         scratch_shapes=[
@@ -491,8 +515,8 @@
             pltpu.VMEM((4, 256, 256), bf16),
             pltpu.VMEM((2, 128, 512), f32),
             pltpu.VMEM((2, COLS, N), f32),
-            pltpu.VMEM((NSPEC * LPROJ, COLS, N), f32),
-            pltpu.VMEM((2, 2 * N, 2 * ATOMS), bf16),
+            pltpu.VMEM((NSPEC * LPROJ, COLS, COLS), f32),
+            pltpu.VMEM((2, 2 * COLS, 2 * ATOMS), bf16),
             pltpu.VMEM((2, COLS, 2 * ATOMS), f32),
             pltpu.VMEM((2, 128, 512), f32),
             pltpu.VMEM((2, COLS, N), f32),
@@ -508,7 +532,7 @@
             pltpu.SemaphoreType.REGULAR,
         ],
         compiler_params=pltpu.CompilerParams(
-            collective_id=0, has_side_effects=True, vmem_limit_bytes=60 * 1024 * 1024
+            collective_id=0, has_side_effects=True, vmem_limit_bytes=57 * 1024 * 1024
         ),
     )(
         psi_coeff,
@@ -519,19 +543,6 @@
         species.reshape(1, ATOMS),
         *consts,
     )
-    return pl.pallas_call(
-        place,
-        out_shape=jax.ShapeDtypeStruct((2, 16, 32, N), f32),
-        in_specs=[hbm],
-        out_specs=hbm,
-        scratch_shapes=[
-            pltpu.VMEM((2, 18, 8, N), f32),
-            pltpu.VMEM((7, 32, N), f32),
-            pltpu.SemaphoreType.DMA,
-            pltpu.SemaphoreType.DMA((16,)),
-        ],
-        compiler_params=pltpu.CompilerParams(vmem_limit_bytes=60 * 1024 * 1024),
-    )(columns)
 
 
 def solution(mesh):

time: 52.5 us -> 49 us (0.933)
  Pallas kernels: 52.3 us -> 47.9 us
  local copies, waits for them, and re-layouts: 0 us -> 0.97 us
    pallas_call x2 -> x1, Pallas kernels: 52.3 us -> 47.9 us  [per_device(): pl.pallas_call(kernel, out_shape=pltpu.VMEM((2, 16, 32, N), f32), in_spec...]
    unnamed x0 -> x1, local copies, waits for them, and re-layouts: none -> 0.97 us
where the time goes in v4:
time: 49 us; the launch traced here: 48.9 us
  Pallas kernels  47.9 us (98%)
  local copies, waits for them, and re-layouts  0.97 us (2%)
    pallas_call x1, Pallas kernels, per_device(): pl.pallas_call(kernel, out_shape=pltpu.VMEM((2, 16, 32, N), f32), in_spec...  47.9 us

profile of v4, /device:TPU:1, one launch (start us, length us, event | category | flops | bytes accessed | tf_op | source)
XLA Modules:
  0.0 48.9 jit_solution(4381758547313249641)
XLA Ops:
  0.0 47.9 %shard_map.109 = f32[2,16,32,256]{3,2,1,0:T(8,128)S(1)} custom-call(f32[2,16,32,256]{3,2,1,0:T(8,128)} %psi_h.1, f32[2,256,256]{2,1,0:T(8,128)} %pot_h.1, bf16[2,3,16,32,256]{4,3,2,1,0:T(8,128)(2,1)} %proj_h.1, f32[3,2,3]{2,1,0:T(2,128)} %bitcast.2, f32[3,64]{1,0:T(4,128)} %pos_h.1, s32[1,64]{1,0:T(1,128)} %bitcast.3, ...), custom_call_target="tpu_custom_call" | custom-call | tf_op jit(solution)/shard_map/pallas_call | solution.py:500
  47.9 1.0 %copy.13 = f32[2,16,32,256]{3,2,1,0:T(8,128)} copy(f32[2,16,32,256]{3,2,1,0:T(8,128)S(1)} %shard_map.109) | data formatting | bytes 2097152

commit v5 on v4

--- a/solution.py
+++ b/solution.py
@@ -150,7 +150,7 @@
     psi, pot, proj, coup, pos, spec, tz, t1, t1t, e, t2,
     xs, pf, pz, pxy, vt, nl,
     zs, r2, s3, r4, ar0, ar1, ar2,
-    load_sem, sems, ready,
+    load_sem, sems,
 ):
     gx = lax.axis_index("gx")
     gy = lax.axis_index("gy")
@@ -176,14 +176,26 @@
     for load in loads[:3]:
         load.start()
     barrier = pltpu.get_barrier_semaphore()
-    for d in range(1, GX):
+    by_x = [lax.rem(gx + d, GX) for d in range(GX)]
+    by_y = [lax.rem(gy + d, GY) for d in range(GY)]
+
+    def greet(px, py):
         pl.semaphore_signal(
-            barrier, inc=1, device_id={"gx": lax.rem(gx + d, GX)}, device_id_type=MESH
+            barrier, inc=1, device_id={"gx": px, "gy": py}, device_id_type=MESH
         )
-    for d in range(1, GY):
-        pl.semaphore_signal(
-            barrier, inc=1, device_id={"gy": lax.rem(gy + d, GY)}, device_id_type=MESH
-        )
+
+    def greet_rows(j):
+        @pl.loop(0, GY)
+        def _(d):
+            py = lax.rem(gy + d, GY)
+            greet(by_x[8 - j], py)
+            if j > 0:
+                greet(by_x[8 + j], py)
+
+    for j in range(8):
+        greet_rows(j)
+    for py in by_y[1:]:
+        greet(gx, py)
     for load in loads[3:]:
         load.start()
 
@@ -219,9 +231,6 @@
 
     def over_y(*args):
         return exchange("gy", gy, GY, *args)
-
-    by_x = [lax.rem(gx + d, GX) for d in range(GX)]
-    by_y = [lax.rem(gy + d, GY) for d in range(GY)]
 
     def exchange_all(slot, source, target, source_at, target_at):
         send_sem, recv_sem = sems.at[2 * slot], sems.at[2 * slot + 1]
@@ -286,8 +295,6 @@
         rows = pl.ds(256 * t, 256)
         return tz[0, rows, :], tz[1, rows, :]
 
-    few_x, few_y = pl.ds(0, GX - 1), pl.ds(0, GY - 1)
-
     def lines(t):
         zs[t] = product(tz_parts(t), x_parts, ((1,), (1,)))
 
@@ -295,11 +302,8 @@
         return exchange_all(t, zs.at[t], r2.at[t], by_gx, by_gy)
 
     lines(0)
-    pl.semaphore_wait(barrier, GX + GY - 2)
-    for py in by_y[1:]:
-        pl.semaphore_signal(ready, inc=1, device_id={"gy": py}, device_id_type=MESH)
     lines(1)
-    pl.semaphore_wait(ready, GY - 1)
+    pl.semaphore_wait(barrier, GX * GY - 1)
     steps, sent1, landed1 = zip(scatter(0), scatter(1))
     queue = [*steps[0], *steps[1]]
 
@@ -357,14 +361,11 @@
             sums.append(jnp.sum(along, axis=0, keepdims=True))
     species = jnp.concatenate([spec[...], spec[...]], axis=1)
     norm = 4.0 / math.sqrt(N * N * N)
-    sub = iota((8, 2 * ATOMS), 0)
-    part = jnp.zeros((8, 2 * ATOMS), jnp.float32)
     for q in range(LPROJ):
-        chosen = jnp.where(species == 0, sums[q], sums[LPROJ + q]) * norm
-        part = jnp.where(sub == q, chosen, part)
-    ar0[0] = part
+        ar0[0, q : q + 1, :] = jnp.where(species == 0, sums[q], sums[LPROJ + q]) * norm
     sent_a1, landed_a1 = over_x(
-        4, lambda p: ar0.at[0], lambda m: ar1.at[m], ar1.at[few_x], ar1
+        4, lambda p: ar0.at[0], lambda m: ar1.at[pl.ds(LPROJ * m, LPROJ), :],
+        ar1.at[pl.ds(0, LPROJ * (GX - 1)), :], ar1,
     )
 
     loads[5].wait()
@@ -423,12 +424,13 @@
     queue += steps4[0]
     proceed(9)
     landed_a1()
-    total = ar1[0]
+    total = ar1[0:LPROJ, :]
     for g in range(1, GX):
-        total += ar1[g]
+        total += ar1[LPROJ * g : LPROJ * (g + 1), :]
     ar0[1] = total
     sent_a2, landed_a2 = over_y(
-        5, lambda p: ar0.at[1], lambda m: ar2.at[m], ar2.at[few_y], ar2
+        5, lambda p: ar0.at[1], lambda m: ar2.at[pl.ds(LPROJ * m, LPROJ), :],
+        ar2.at[pl.ds(0, LPROJ * (GY - 1)), :], ar2,
     )
     proceed(9)
     plane(1)
@@ -437,9 +439,9 @@
     proceed(9)
 
     landed_a2()
-    total = ar2[0]
+    total = ar2[0:LPROJ, :]
     for g in range(1, GY):
-        total += ar2[g]
+        total += ar2[LPROJ * g : LPROJ * (g + 1), :]
     spread = []
     for s in range(NSPEC):
         for q in range(LPROJ):
@@ -524,12 +526,11 @@
             pltpu.VMEM((2, 256, COLS), f32),
             pltpu.VMEM((2, 256, COLS), f32),
             pltpu.VMEM((2, 256, COLS), f32),
-            pltpu.VMEM((2, 8, 128), f32),
-            pltpu.VMEM((GX, 8, 128), f32),
-            pltpu.VMEM((GY, 8, 128), f32),
+            pltpu.VMEM((2, LPROJ, 128), f32),
+            pltpu.VMEM((GX * LPROJ, 128), f32),
+            pltpu.VMEM((GY * LPROJ, 128), f32),
             pltpu.SemaphoreType.DMA((14,)),
             pltpu.SemaphoreType.DMA((12,)),
-            pltpu.SemaphoreType.REGULAR,
         ],
         compiler_params=pltpu.CompilerParams(
             collective_id=0, has_side_effects=True, vmem_limit_bytes=57 * 1024 * 1024

time: 49 us -> 48.2 us (0.984)
  Pallas kernels: 47.9 us -> 47.1 us
    pallas_call x1, Pallas kernels: 47.9 us -> 47.1 us  [per_device(): pl.pallas_call(kernel, out_shape=pltpu.VMEM((2, 16, 32, N), f32), in_spec...]
where the time goes in v5:
time: 48.2 us; the launch traced here: 48.1 us
  Pallas kernels  47.1 us (98%)
  local copies, waits for them, and re-layouts  0.97 us (2%)
    pallas_call x1, Pallas kernels, per_device(): pl.pallas_call(kernel, out_shape=pltpu.VMEM((2, 16, 32, N), f32), in_spec...  47.1 us
    unnamed x1, local copies, waits for them, and re-layouts  0.97 us

profile of v5, /device:TPU:1, one launch (start us, length us, event | category | flops | bytes accessed | tf_op | source)
XLA Modules:
  0.0 48.1 jit_solution(10861103224903251586)
XLA Ops:
  0.0 47.1 %shard_map.109 = f32[2,16,32,256]{3,2,1,0:T(8,128)S(1)} custom-call(f32[2,16,32,256]{3,2,1,0:T(8,128)} %psi_h.1, f32[2,256,256]{2,1,0:T(8,128)} %pot_h.1, bf16[2,3,16,32,256]{4,3,2,1,0:T(8,128)(2,1)} %proj_h.1, f32[3,2,3]{2,1,0:T(2,128)} %bitcast.2, f32[3,64]{1,0:T(4,128)} %pos_h.1, s32[1,64]{1,0:T(1,128)} %bitcast.3, ...), custom_call_target="tpu_custom_call" | custom-call | tf_op jit(solution)/shard_map/pallas_call | solution.py:502
  47.1 1.0 %copy.13 = f32[2,16,32,256]{3,2,1,0:T(8,128)} copy(f32[2,16,32,256]{3,2,1,0:T(8,128)S(1)} %shard_map.109) | data formatting | bytes 2097152

commit v6 on v5

--- a/solution.py
+++ b/solution.py
@@ -302,7 +302,6 @@
         return exchange_all(t, zs.at[t], r2.at[t], by_gx, by_gy)
 
     lines(0)
-    lines(1)
     pl.semaphore_wait(barrier, GX * GY - 1)
     steps, sent1, landed1 = zip(scatter(0), scatter(1))
     queue = [*steps[0], *steps[1]]
@@ -311,7 +310,8 @@
         for _ in range(min(count, len(queue))):
             queue.pop(0)()
 
-    proceed(3)
+    proceed(5)
+    lines(1)
     for c in range(2):
         for row in range(16):
             if row in ROWS_X:

time: 48.2 us -> 47.7 us (0.990)
  Pallas kernels: 47.1 us -> 46.6 us
where the time goes in v6:
time: 47.7 us; the launch traced here: 47.6 us
  Pallas kernels  46.6 us (98%)
  local copies, waits for them, and re-layouts  0.97 us (2%)
    pallas_call x1, Pallas kernels, per_device(): pl.pallas_call(kernel, out_shape=pltpu.VMEM((2, 16, 32, N), f32), in_spec...  46.6 us
    unnamed x1, local copies, waits for them, and re-layouts  0.97 us

profile of v6, /device:TPU:1, one launch (start us, length us, event | category | flops | bytes accessed | tf_op | source)
XLA Modules:
  0.0 47.6 jit_solution(10301566081420087620)
XLA Ops:
  0.0 46.6 %shard_map.109 = f32[2,16,32,256]{3,2,1,0:T(8,128)S(1)} custom-call(f32[2,16,32,256]{3,2,1,0:T(8,128)} %psi_h.1, f32[2,256,256]{2,1,0:T(8,128)} %pot_h.1, bf16[2,3,16,32,256]{4,3,2,1,0:T(8,128)(2,1)} %proj_h.1, f32[3,2,3]{2,1,0:T(2,128)} %bitcast.2, f32[3,64]{1,0:T(4,128)} %pos_h.1, s32[1,64]{1,0:T(1,128)} %bitcast.3, ...), custom_call_target="tpu_custom_call" | custom-call | tf_op jit(solution)/shard_map/pallas_call | solution.py:502
  46.6 1.0 %copy.13 = f32[2,16,32,256]{3,2,1,0:T(8,128)} copy(f32[2,16,32,256]{3,2,1,0:T(8,128)S(1)} %shard_map.109) | data formatting | bytes 2097152
